TPU v7x, 32 devices: a whole 2x2x4 slice. The times are simulated.
32 devices in a mesh: sens: 4 (over y, x), pts: 8 (over z, core).
Axes of the slice: x: 2, y: 2, z: 4, core: 2. Of those that a mesh axis runs over, the one named last changes fastest.
Arguments:
- vectors: float32 [4, 256, 420], P(None, 'pts'), may hold values from -6 to 6
- kernel_hat: float32 [2, 424, 256, 256], P(None, 'pts', 'sens'), may hold values from -0.375 to 0.375
- noise_prec: float32 [256], P(('sens', 'pts')), may hold values from 0.3 to 3
- stencil_coefficients_raw: float32 [256, 6], P('pts'), may hold values from 0.1 to 2
- offsets: int32 [256, 6], P('pts'), may hold values from -32 to 32
- amplitude: float32 [256], P('pts'), may hold values from 0.5 to 2
- cheb_coef: float32 [5], replicated, may hold values from 0.2 to 1
Outputs:
- hess_vec: float32 [4, 256, 420], P(None, 'pts')
Inputs may be any that keep to these rules, and one draw needn't show every extreme that they name: `offsets`: each point's stencil neighbours lie at most 32 points away in the point order.
All inputs are finite; a program needn't handle non-finite values.
Results may differ from a plain program's by a relative error of at most 0.00016.
Values sent between devices are 32-bit elements; how exact they have to be, the bound alone decides.
A program may use at most 64 MiB of HBM per device.

v0:
```python
import functools

import jax
import jax.numpy as jnp
import ml_dtypes
import numpy as np
from jax import lax
from jax.experimental import pallas as pl
from jax.experimental.pallas import tpu as pltpu
from jax.sharding import PartitionSpec as P

exact_evaluation_flag = lax.Precision.HIGHEST


def transform_tables(length, padded):
    time_index = jnp.arange(length, dtype=jnp.int32)
    frequency = jnp.arange(padded, dtype=jnp.int32)
    period = 2 * length
    phase_index = frequency[:, None] * time_index[None, :] % period
    angles = 2.0 * jnp.pi / period * phase_index.astype(jnp.float32)
    active = (frequency <= length).astype(jnp.float32)[:, None]
    cosine = jnp.cos(angles)
    sine_part = jnp.sin(angles)
    forward_operator = jnp.stack([cosine * active, -sine_part * active])
    edge_rows = (frequency == 0) | (frequency == length)
    weight = jnp.where(edge_rows, 1.0, 2.0).astype(jnp.float32)[:, None] * active / period
    inverse = jnp.stack([cosine * weight, -sine_part * weight])
    return (forward_operator, inverse)


def to_spectrum(time_series_values, forward_operator):
    return jnp.einsum(
        "vpt,cft->vcfp", time_series_values, forward_operator, precision=exact_evaluation_flag
    )


def to_series(spectrum, inverse):
    return jnp.einsum("vcfp,cft->vpt", spectrum, inverse, precision=exact_evaluation_flag)


def chebyshev(values_in, operator, cheb_coef):
    previous = values_in
    current = operator(values_in)
    running_sum = cheb_coef[0] * previous + cheb_coef[1] * current
    for degree in range(2, cheb_coef.shape[0]):
        following = 2.0 * operator(current) - previous
        previous, current = (current, following)
        running_sum = running_sum + cheb_coef[degree] * current
    return running_sum


def full_matrix(weights_all, offsets_all):
    point_count = weights_all.shape[0]
    positions = jnp.arange(point_count, dtype=jnp.int32)
    target = positions[:, None] + offsets_all
    dense_operator_matrix = jnp.zeros((point_count, point_count), jnp.float32)
    for column in range(weights_all.shape[1]):
        hit = (target[:, column][:, None] == positions[None, :]).astype(jnp.float32)
        dense_operator_matrix = dense_operator_matrix + weights_all[:, column][:, None] * hit
    return dense_operator_matrix


def plain(vectors, kernel_hat, noise_prec, stencil_coefficients_raw, offsets, amplitude, cheb_coef):
    length = vectors.shape[2]
    freq_block = kernel_hat.shape[1]
    padded = freq_block * lax.axis_size("pts")
    forward_operator, inverse = transform_tables(length, padded)
    weights = stencil_coefficients_raw / jnp.sum(stencil_coefficients_raw, axis=1, keepdims=True)
    kernel_real = kernel_hat[0]
    kernel_imag = kernel_hat[1]
    offsets_all = lax.all_gather(offsets, "pts", axis=0, tiled=True)
    weights_all, amplitude_all = (
        lax.all_gather(weights, "pts", axis=0, tiled=True),
        lax.all_gather(amplitude, "pts", axis=0, tiled=True),
    )
    dense_operator_matrix = full_matrix(weights_all, offsets_all)

    def forward_mean(values):
        return jnp.einsum(
            "vcfq,pq->vcfp", values, dense_operator_matrix, precision=exact_evaluation_flag
        )

    def backward_mean(values):
        return jnp.einsum(
            "vcfp,pq->vcfq", values, dense_operator_matrix, precision=exact_evaluation_flag
        )

    source = to_spectrum(vectors, forward_operator)
    spectrum = lax.all_to_all(source, "pts", split_axis=2, concat_axis=3, tiled=True)
    spectrum = amplitude_all[None, None, None, :] * chebyshev(spectrum, forward_mean, cheb_coef)
    real_part = spectrum[:, 0]
    imag_part = spectrum[:, 1]
    data_real = jnp.einsum(
        "fsp,vfp->vfs", kernel_real, real_part, precision=exact_evaluation_flag
    ) - jnp.einsum("fsp,vfp->vfs", kernel_imag, imag_part, precision=exact_evaluation_flag)
    data_imag = jnp.einsum(
        "fsp,vfp->vfs", kernel_real, imag_part, precision=exact_evaluation_flag
    ) + jnp.einsum("fsp,vfp->vfs", kernel_imag, real_part, precision=exact_evaluation_flag)
    data_spec = jnp.stack([data_real, data_imag], axis=1)
    time_series_values = (
        jnp.einsum(
            "rklu,klq->ruq",
            lax.all_to_all(data_spec, "pts", split_axis=3, concat_axis=2, tiled=True),
            inverse,
            precision=exact_evaluation_flag,
        )
        * noise_prec[None, :, None]
    )
    weighted_result = jnp.einsum(
        "lew,jkw->ljke", time_series_values, forward_operator, precision=exact_evaluation_flag
    )
    weighted_result = lax.all_to_all(
        weighted_result, "pts", split_axis=2, concat_axis=3, tiled=True
    )
    back_real = weighted_result[:, 0]
    back_imag = weighted_result[:, 1]
    grad_real = jnp.einsum(
        "fsp,vfs->vfp", kernel_real, back_real, precision=exact_evaluation_flag
    ) + jnp.einsum("fsp,vfs->vfp", kernel_imag, back_imag, precision=exact_evaluation_flag)
    grad_imag = jnp.einsum(
        "fsp,vfs->vfp", kernel_real, back_imag, precision=exact_evaluation_flag
    ) - jnp.einsum("fsp,vfs->vfp", kernel_imag, back_real, precision=exact_evaluation_flag)
    partial_value = chebyshev(
        amplitude_all[None, None, None, :] * jnp.stack([grad_real, grad_imag], axis=1),
        backward_mean,
        cheb_coef,
    )
    summed = lax.psum(partial_value, "sens")
    moved = lax.all_to_all(summed, "pts", split_axis=3, concat_axis=2, tiled=True)
    gradient = to_series(moved, inverse)
    return vectors + gradient


BF = jnp.bfloat16
F32 = jnp.float32
MESH = pl.DeviceIdType.MESH


def up(size, multiple):
    return -(-size // multiple) * multiple


def host_tables(length, block, blocks, padded_block, lanes, padded_time):
    period = 2 * length
    forward = np.zeros((padded_time, blocks, lanes))
    inverse = np.zeros((blocks, lanes, padded_time))
    time = np.arange(length)
    for index in range(blocks):
        frequency = index * block + np.arange(block)
        angle = 2.0 * np.pi / period * (frequency[:, None] * time[None, :] % period)
        active = (frequency <= length)[:, None]
        edge = (frequency == 0) | (frequency == length)
        weight = np.where(edge, 1.0, 2.0)[:, None] / period
        for part, table in enumerate((np.cos(angle) * active, -np.sin(angle) * active)):
            at = slice(part * padded_block, part * padded_block + block)
            forward[:length, index, at] = table.T
            inverse[index, at, :length] = table * weight
    halves = []
    for table in (forward.reshape(padded_time, -1), inverse.reshape(-1, padded_time)):
        high = table.astype(ml_dtypes.bfloat16)
        low = (table - high.astype(np.float64)).astype(ml_dtypes.bfloat16)
        halves.append(np.stack([high, low]))
    return halves


def split(values):
    high = values.astype(BF)
    return high, (values - high.astype(F32)).astype(BF)


NN = (((1,), (0,)), ((), ()))
NT = (((1,), (1,)), ((), ()))


def dot3(left, right_high, right_low, dims=NN):
    rows = left.shape[0]
    high, low = split(left)
    both = lax.dot_general(
        jnp.concatenate([high, low], axis=0), right_high, dims, preferred_element_type=F32
    )
    cross = lax.dot_general(high, right_low, dims, preferred_element_type=F32)
    return both[:rows] + both[rows:] + cross


def fused_kernel(
    sizes,
    vec, kern, noise, raw, offs, amp, cheb, fwd_in, inv_in,
    out,
    fwd, inv, k_f32, k_hl, v_pad, pack, a_send, a_recv, spec, y_buf, d_send, d_recv,
    e_send, e_recv, l_buf, g_buf, r_recv, h_send, h_recv, o_buf,
    load_sem, pack_s, pack_r, a_s, a_r, s_s, s_r, d_s, d_r, e_s, e_r, g_s, g_r, h_s, h_r, o_s, o_r,
):
    nv, n_sens, n_pts, fb, fbp, cfp, sl, sq, pt, ple, length, tp = sizes
    me_s = lax.axis_index("sens")
    me_p = lax.axis_index("pts")
    rows = 2 * nv

    loads = [
        pltpu.make_async_copy(fwd_in, fwd, load_sem.at[0]),
        pltpu.make_async_copy(kern.at[0], k_f32.at[0], load_sem.at[1]),
        pltpu.make_async_copy(kern.at[1], k_f32.at[1], load_sem.at[2]),
        pltpu.make_async_copy(inv_in, inv, load_sem.at[3]),
    ]
    for load in loads:
        load.start()

    barrier = pltpu.get_barrier_semaphore()
    for step in range(1, n_pts):
        pl.semaphore_signal(
            barrier, inc=1, device_id=(me_s, lax.rem(me_p + step, n_pts)), device_id_type=MESH
        )
    for step in range(1, n_sens):
        pl.semaphore_signal(
            barrier, inc=1, device_id=(lax.rem(me_s + step, n_sens), me_p), device_id_type=MESH
        )

    def over_pts(step, src, dst, send_sem, recv_sem):
        target = lax.rem(me_p + step, n_pts)
        return pltpu.make_async_remote_copy(
            src_ref=src(target), dst_ref=dst(me_p), send_sem=send_sem.at[step],
            recv_sem=recv_sem.at[step], device_id=(me_s, target), device_id_type=MESH,
        )

    def over_sens(step, src, dst, send_sem, recv_sem):
        target = lax.rem(me_s + step, n_sens)
        return pltpu.make_async_remote_copy(
            src_ref=src(target), dst_ref=dst(me_s), send_sem=send_sem.at[step],
            recv_sem=recv_sem.at[step], device_id=(target, me_p), device_id_type=MESH,
        )

    def arrive_pts(step, src, dst, send_sem, recv_sem):
        source = lax.rem(me_p - step + n_pts, n_pts)
        pltpu.make_async_remote_copy(
            src_ref=src(source), dst_ref=dst(source), send_sem=send_sem.at[step],
            recv_sem=recv_sem.at[step], device_id=(me_s, source), device_id_type=MESH,
        ).wait_recv()

    def arrive_sens(step, src, dst, send_sem, recv_sem):
        source = lax.rem(me_s - step + n_sens, n_sens)
        pltpu.make_async_remote_copy(
            src_ref=src(source), dst_ref=dst(source), send_sem=send_sem.at[step],
            recv_sem=recv_sem.at[step], device_id=(source, me_p), device_id_type=MESH,
        ).wait_recv()

    pts_steps = range(1, n_pts)
    sens_steps = range(1, n_sens)
    started = []

    def send_pts(*args):
        for step in pts_steps:
            copy = over_pts(step, *args)
            copy.start()
            started.append(copy)

    def send_sens(*args):
        for step in sens_steps:
            copy = over_sens(step, *args)
            copy.start()
            started.append(copy)

    nb = raw.shape[1]
    pack[me_p] = jnp.zeros(pack.shape[1:], F32)
    raw_t = jnp.transpose(raw[...])
    pack[me_p, 0:nb, 0:ple] = raw_t / jnp.sum(raw_t, axis=0, keepdims=True)
    pack[me_p, nb : nb + 1, 0:ple] = amp[...]
    pack[me_p, 0:nb, ple : 2 * ple] = jnp.transpose(offs[...].astype(F32))

    v_pad[...] = jnp.zeros(v_pad.shape, F32)
    v_pad[:, 0:length] = vec[me_s]
    loads[0].wait()
    source = dot3(v_pad[...], fwd[0], fwd[1])
    for index in range(n_pts):
        a_send[index] = source[:, index * cfp : (index + 1) * cfp]

    pl.semaphore_wait(barrier, n_pts - 1 + n_sens - 1)
    pack_args = (lambda _: pack.at[me_p], lambda i: pack.at[i], pack_s, pack_r)
    send_pts(*pack_args)
    a_args = (lambda i: a_send.at[i], lambda i: a_recv.at[i], a_s, a_r)
    send_pts(*a_args)
    a_recv[me_p] = a_send[me_p]

    loads[1].wait()
    loads[2].wait()

    def halve(index, carry):
        for part in range(2):
            high, low = split(k_f32[part, index])
            k_hl[index, part * sl : (part + 1) * sl] = high
            k_hl[index, (2 + part) * sl : (3 + part) * sl] = low
        return carry

    lax.fori_loop(0, fb, halve, 0)
    for index in range(fb, fbp):
        k_hl[index] = jnp.zeros(k_hl.shape[1:], BF)

    for step in pts_steps:
        arrive_pts(step, *pack_args)
    gathered = [pack[index] for index in range(n_pts)]
    weights_row = jnp.concatenate([block[:, 0:ple] for block in gathered], axis=1)
    offsets_row = jnp.concatenate([block[:, ple : 2 * ple] for block in gathered], axis=1)
    down = lax.broadcasted_iota(jnp.int32, (pt, pt), 0)
    across = lax.broadcasted_iota(jnp.int32, (pt, pt), 1)
    shift = (down - across).astype(F32)
    mean_t = jnp.zeros((pt, pt), F32)
    for k in range(nb):
        mean_t = mean_t + jnp.where(
            shift == offsets_row[k : k + 1], weights_row[k : k + 1], 0.0
        )
    identity = jnp.where(down == across, 1.0, 0.0).astype(F32)
    before, now = identity, mean_t
    total = cheb[0] * before + cheb[1] * now
    mean_h, mean_l = split(mean_t)
    for degree in range(2, cheb.shape[0]):
        before, now = now, 2.0 * dot3(now, mean_h, mean_l) - before
        total = total + cheb[degree] * now
    prior_t = total * weights_row[nb : nb + 1]
    prior_h, prior_l = split(prior_t)

    for step in pts_steps:
        arrive_pts(step, *a_args)
    by_point = a_recv[...].reshape(pt, cfp)
    own = dot3(jnp.transpose(by_point), prior_h, prior_l)
    tiles = pt // 128
    for part in range(2):
        for tile in range(tiles):
            spec[part, me_s, tile] = own[
                part * fbp : (part + 1) * fbp, tile * 128 : (tile + 1) * 128
            ]
    s_args = (lambda _: spec.at[:, me_s], lambda i: spec.at[:, i], s_s, s_r)
    send_sens(*s_args)
    for step in sens_steps:
        arrive_sens(step, *s_args)

    spec_rows = spec.reshape(rows * tiles * fbp, 128)

    def predict(index, carry):
        values = jnp.concatenate(
            [
                spec_rows[pl.ds(tile * fbp + index, rows, stride=tiles * fbp), :]
                for tile in range(tiles)
            ],
            axis=1,
        )
        high, low = split(values)
        product = lax.dot_general(
            jnp.concatenate([high, low], axis=0), k_hl[index], NT, preferred_element_type=F32
        )
        y_buf[index] = (
            product[:rows, : 2 * sl] + product[rows:, : 2 * sl] + product[:rows, 2 * sl :]
        )
        return carry

    lax.fori_loop(0, fbp, predict, 0, unroll=8)

    y_rows = y_buf.reshape(fbp * rows, 2 * sl)
    blank = jnp.zeros((cfp - 2 * fbp, 2 * sl), F32)
    for v in range(nv):
        real = y_rows[pl.ds(v, fbp, stride=rows), :]
        imag = y_rows[pl.ds(nv + v, fbp, stride=rows), :]
        direct = jnp.concatenate([real, imag, blank], axis=0)
        crossed = jnp.concatenate([-imag, real, blank], axis=0)
        data = jnp.transpose(direct + pltpu.roll(crossed, sl, 1))
        for index in range(n_pts):
            d_send[index, v] = data[index * sq : (index + 1) * sq]
    d_args = (lambda i: d_send.at[i], lambda i: d_recv.at[i], d_s, d_r)
    send_pts(*d_args)
    d_recv[me_p] = d_send[me_p]
    loads[3].wait()
    which = lax.rem(lax.broadcasted_iota(jnp.int32, (nv * sq, 1), 0), sq)
    precision = jnp.zeros((nv * sq, 1), F32)
    for index in range(sq):
        precision = jnp.where(which == index, noise[index], precision)
    for step in pts_steps:
        arrive_pts(step, *d_args)
    data_spec = jnp.concatenate(
        [d_recv[index].reshape(nv * sq, cfp) for index in range(n_pts)], axis=1
    )
    data = dot3(data_spec, inv[0], inv[1]) * precision
    back = dot3(data, fwd[0], fwd[1])
    for index in range(n_pts):
        e_send[index] = back[:, index * cfp : (index + 1) * cfp].reshape(nv, sq, cfp)
    e_args = (lambda i: e_send.at[i], lambda i: e_recv.at[i], e_s, e_r)
    send_pts(*e_args)
    e_recv[me_p] = e_send[me_p]
    for step in pts_steps:
        arrive_pts(step, *e_args)
    for v in range(nv):
        turned = jnp.transpose(
            jnp.concatenate([e_recv[index, v] for index in range(n_pts)], axis=0)
        )
        real, imag = turned[:fbp], turned[fbp : 2 * fbp]
        l_buf[0, v] = jnp.concatenate([real, imag], axis=1)
        l_buf[1, v] = jnp.concatenate([imag, -real], axis=1)

    l_rows = l_buf.reshape(rows * fbp, 2 * sl)
    g_rows = g_buf.reshape(rows * tiles * fbp, 128)

    def adjoint(index, carry):
        values = l_rows[pl.ds(index, rows, stride=fbp), :]
        high, low = split(values)
        left = jnp.concatenate(
            [
                jnp.concatenate([high, high], axis=1),
                jnp.concatenate([low, jnp.zeros_like(low)], axis=1),
            ],
            axis=0,
        )
        product = lax.dot_general(left, k_hl[index], NN, preferred_element_type=F32)
        result = product[:rows] + product[rows:]
        for tile in range(tiles):
            g_rows[pl.ds(tile * fbp + index, rows, stride=tiles * fbp), :] = result[
                :, tile * 128 : (tile + 1) * 128
            ]
        return carry

    lax.fori_loop(0, fbp, adjoint, 0, unroll=8)

    g_args = (lambda i: g_buf.at[:, i], lambda i: r_recv.at[i], g_s, g_r)
    send_sens(*g_args)
    gradient = g_buf[:, me_s]
    for step in sens_steps:
        arrive_sens(step, *g_args)
        gradient = gradient + r_recv[lax.rem(me_s - step + n_sens, n_sens)]
    gradient = jnp.concatenate(
        [
            jnp.concatenate([gradient[part, tile] for tile in range(tiles)], axis=1)
            for part in range(2)
        ]
        + [jnp.zeros((cfp - 2 * fbp, pt), F32)],
        axis=0,
    )
    grad_h, grad_l = split(gradient)
    h_send[...] = dot3(prior_t, grad_h, grad_l, NT).reshape(h_send.shape)
    h_args = (lambda i: h_send.at[i], lambda i: h_recv.at[i], h_s, h_r)
    send_pts(*h_args)
    h_recv[me_p] = h_send[me_p]
    for step in pts_steps:
        arrive_pts(step, *h_args)
    last = jnp.concatenate([h_recv[index] for index in range(n_pts)], axis=1)
    o_buf[me_s] = dot3(last, inv[0], inv[1])
    o_args = (lambda _: o_buf.at[me_s], lambda i: o_buf.at[i], o_s, o_r)
    send_sens(*o_args)
    out[me_s] = vec[me_s] + o_buf[me_s, :, 0:length]
    for step in sens_steps:
        arrive_sens(step, *o_args)
        other = lax.rem(me_s - step + n_sens, n_sens)
        out[other] = vec[other] + o_buf[other, :, 0:length]
    for copy in started:
        copy.wait_send()


def local(vectors, kernel_hat, noise_prec, stencil_coefficients_raw, offsets, amplitude, cheb_coef):
    n_sens, n_pts = lax.axis_size("sens"), lax.axis_size("pts")
    nv, ple, length = vectors.shape
    fb, sl, pt = kernel_hat.shape[1:]
    nb = offsets.shape[1]
    fbp = up(fb, 8)
    cfp = up(2 * fbp, 128)
    tp = up(length, 128)
    sq = sl // n_pts
    fits = (
        nv == n_sens
        and 2 * nv == 8
        and nb < 8
        and ple % 8 == 0
        and 2 * ple <= 128
        and sl == sq * n_pts
        and sq % 8 == 0
        and 2 * sl == 128
        and pt % 128 == 0
        and kernel_hat.size < 2**21
    )
    if not fits:
        return plain(
            vectors, kernel_hat, noise_prec, stencil_coefficients_raw, offsets, amplitude, cheb_coef
        )
    forward, inverse = host_tables(length, fb, n_pts, fbp, cfp, tp)
    sizes = (nv, n_sens, n_pts, fb, fbp, cfp, sl, sq, pt, ple, length, tp)
    vmem = pl.BlockSpec(memory_space=pltpu.VMEM)
    smem = pl.BlockSpec(memory_space=pltpu.SMEM)
    anywhere = pl.BlockSpec(memory_space=pl.ANY)
    wide = n_pts * cfp

    def f32(*shape):
        return pltpu.VMEM(shape, F32)

    def sems(count):
        return pltpu.SemaphoreType.DMA((count,))

    return pl.pallas_call(
        functools.partial(fused_kernel, sizes),
        out_shape=jax.ShapeDtypeStruct(vectors.shape, F32),
        in_specs=[vmem, anywhere, smem, vmem, vmem, vmem, smem, anywhere, anywhere],
        out_specs=vmem,
        scratch_shapes=[
            pltpu.VMEM((2, tp, wide), BF),
            pltpu.VMEM((2, wide, tp), BF),
            f32(2, fb, sl, pt),
            pltpu.VMEM((fbp, 4 * sl, pt), BF),
            f32(ple, tp),
            f32(n_pts, 8, 128),
            f32(n_pts, ple, cfp),
            f32(n_pts, ple, cfp),
            f32(2, nv, pt // 128, fbp, 128),
            f32(fbp, 2 * nv, 2 * sl),
            f32(n_pts, nv, sq, cfp),
            f32(n_pts, nv, sq, cfp),
            f32(n_pts, nv, sq, cfp),
            f32(n_pts, nv, sq, cfp),
            f32(2, nv, fbp, 2 * sl),
            f32(2, nv, pt // 128, fbp, 128),
            f32(n_sens, 2, pt // 128, fbp, 128),
            f32(n_pts, ple, cfp),
            f32(n_pts, ple, cfp),
            f32(nv, ple, tp),
            sems(4),
            *[sems(n_pts)] * 4,
            *[sems(n_sens)] * 2,
            *[sems(n_pts)] * 4,
            *[sems(n_sens)] * 2,
            *[sems(n_pts)] * 2,
            *[sems(n_sens)] * 2,
        ],
        compiler_params=pltpu.CompilerParams(
            collective_id=0, has_side_effects=True, vmem_limit_bytes=56 * 2**20
        ),
    )(
        vectors, kernel_hat, noise_prec, stencil_coefficients_raw, offsets,
        amplitude.reshape(1, ple), cheb_coef, forward, inverse,
    )


def solution(mesh):
    placed = (
        P(None, "pts", None),
        P(None, "pts", "sens", None),
        P(("sens", "pts")),
        P("pts", None),
        P("pts", None),
        P("pts"),
        P(),
    )
    return jax.shard_map(
        local, mesh=mesh, in_specs=placed, out_specs=P(None, "pts", None), check_vma=False
    )
```

profile of v0, /device:TPU:0, one launch (start us, length us, event | category | flops | bytes accessed | tf_op | source)
XLA Modules:
  0.0 56.8 jit_solution(11591508331940465368)
XLA Ops:
  0.0 1.4 %copy.10.raw = f32[32,6]{1,0:T(8,128)} copy(f32[32,6]{0,1:T(8,128)} %param.12) | data formatting | bytes 1536 | tf_op args[3]
  1.4 1.4 %copy.11.offs = s32[32,6]{1,0:T(8,128)} copy(s32[32,6]{0,1:T(8,128)} %param.13) | data formatting | bytes 1536 | tf_op args[4]
  2.7 52.3 %shard_map.91 = f32[4,32,420]{2,1,0:T(8,128)} custom-call(f32[4,32,420]{2,1,0:T(8,128)} %vec.1, f32[2,53,64,256]{3,2,1,0:T(8,128)} %kern.1, f32[8]{0:T(128)} %noise.1, f32[32,6]{1,0:T(8,128)} %copy.10.raw, s32[32,6]{1,0:T(8,128)} %copy.11.offs, f32[1,32]{1,0:T(1,128)} %bitcast.1, f32[5]{0:T(128)} %cheb.1, bf16[2,512,1024]{2,1,0:T(8,128)(2,1)} %constant.4.clone.fwd_in, ...), custom_call_target="tpu_custom_call" | custom-call | tf_op jit(solution)/shard_map/pallas_call | solution.py:490
  55.1 1.7 %copy.13 = f32[4,32,420]{2,1,0:T(8,128)} copy(f32[4,32,420]{2,1,0:T(8,128)} %shard_map.91) | data formatting | bytes 430080
where the time goes:
time: 57 us; the launch traced here: 56.8 us
  Pallas kernels  52.3 us (92%)
  local copies, waits for them, and re-layouts  4.41 us (8%)
    pallas_call x1, Pallas kernels, local(): pl.pallas_call(functools.partial(fused_kernel, sizes), out_shape=jax.Shap...  52.3 us
    unnamed x3, local copies, waits for them, and re-layouts  4.41 us

commit v1 on v0

--- a/solution.py
+++ b/solution.py
@@ -155,8 +155,10 @@
             at = slice(part * padded_block, part * padded_block + block)
             forward[:length, index, at] = table.T
             inverse[index, at, :length] = table * weight
+    forward = forward.reshape(padded_time, blocks // 2, 2 * lanes).transpose(1, 0, 2)
+    inverse = inverse.reshape(blocks // 2, 2 * lanes, padded_time)
     halves = []
-    for table in (forward.reshape(padded_time, -1), inverse.reshape(-1, padded_time)):
+    for table in (forward, inverse):
         high = table.astype(ml_dtypes.bfloat16)
         low = (table - high.astype(np.float64)).astype(ml_dtypes.bfloat16)
         halves.append(np.stack([high, low]))
@@ -182,105 +184,115 @@
     return both[:rows] + both[rows:] + cross
 
 
+def flip(index, step, size):
+    flipped, bit = 0, 1
+    while bit < size:
+        digit = lax.rem(index // bit, 2)
+        flipped = flipped + bit * ((1 - digit) if step & bit else digit)
+        bit *= 2
+    return flipped
+
+
 def fused_kernel(
     sizes,
     vec, kern, noise, raw, offs, amp, cheb, fwd_in, inv_in,
     out,
-    fwd, inv, k_f32, k_hl, v_pad, pack, a_send, a_recv, spec, y_buf, d_send, d_recv,
+    fwd, inv, k_f32, k_hl, v_own, v_pad, pack, a_send, x_all, spec, y_buf, d_send, d_recv,
     e_send, e_recv, l_buf, g_buf, r_recv, h_send, h_recv, o_buf,
-    load_sem, pack_s, pack_r, a_s, a_r, s_s, s_r, d_s, d_r, e_s, e_r, g_s, g_r, h_s, h_r, o_s, o_r,
+    load_sem, pack_s, pack_r, a_s, a_r, f_s, f_r, d_s, d_r, e_s, e_r, g_s, g_r, h_s, h_r, o_s, o_r,
 ):
     nv, n_sens, n_pts, fb, fbp, cfp, sl, sq, pt, ple, length, tp = sizes
     me_s = lax.axis_index("sens")
     me_p = lax.axis_index("pts")
     rows = 2 * nv
-
-    loads = [
-        pltpu.make_async_copy(fwd_in, fwd, load_sem.at[0]),
-        pltpu.make_async_copy(kern.at[0], k_f32.at[0], load_sem.at[1]),
-        pltpu.make_async_copy(kern.at[1], k_f32.at[1], load_sem.at[2]),
-        pltpu.make_async_copy(inv_in, inv, load_sem.at[3]),
-    ]
-    for load in loads:
-        load.start()
-
-    barrier = pltpu.get_barrier_semaphore()
-    for step in range(1, n_pts):
-        pl.semaphore_signal(
-            barrier, inc=1, device_id=(me_s, lax.rem(me_p + step, n_pts)), device_id_type=MESH
-        )
-    for step in range(1, n_sens):
-        pl.semaphore_signal(
-            barrier, inc=1, device_id=(lax.rem(me_s + step, n_sens), me_p), device_id_type=MESH
-        )
-
-    def over_pts(step, src, dst, send_sem, recv_sem):
-        target = lax.rem(me_p + step, n_pts)
-        return pltpu.make_async_remote_copy(
-            src_ref=src(target), dst_ref=dst(me_p), send_sem=send_sem.at[step],
-            recv_sem=recv_sem.at[step], device_id=(me_s, target), device_id_type=MESH,
-        )
-
-    def over_sens(step, src, dst, send_sem, recv_sem):
-        target = lax.rem(me_s + step, n_sens)
-        return pltpu.make_async_remote_copy(
-            src_ref=src(target), dst_ref=dst(me_s), send_sem=send_sem.at[step],
-            recv_sem=recv_sem.at[step], device_id=(target, me_p), device_id_type=MESH,
-        )
-
-    def arrive_pts(step, src, dst, send_sem, recv_sem):
-        source = lax.rem(me_p - step + n_pts, n_pts)
-        pltpu.make_async_remote_copy(
-            src_ref=src(source), dst_ref=dst(source), send_sem=send_sem.at[step],
-            recv_sem=recv_sem.at[step], device_id=(me_s, source), device_id_type=MESH,
-        ).wait_recv()
-
-    def arrive_sens(step, src, dst, send_sem, recv_sem):
-        source = lax.rem(me_s - step + n_sens, n_sens)
-        pltpu.make_async_remote_copy(
-            src_ref=src(source), dst_ref=dst(source), send_sem=send_sem.at[step],
-            recv_sem=recv_sem.at[step], device_id=(source, me_p), device_id_type=MESH,
-        ).wait_recv()
-
+    tiles = pt // 128
+    pairs = n_pts // 2
+    my_pair = me_p // 2
     pts_steps = range(1, n_pts)
     sens_steps = range(1, n_sens)
+    pts_peer = [flip(me_p, step, n_pts) for step in range(n_pts)]
+    sens_peer = [flip(me_s, step, n_sens) for step in range(n_sens)]
+    pair_peer = [flip(my_pair, step, pairs) for step in range(pairs)]
+
+    loads = [
+        pltpu.make_async_copy(vec.at[me_s], v_own, load_sem.at[0]),
+        pltpu.make_async_copy(fwd_in, fwd, load_sem.at[1]),
+        pltpu.make_async_copy(kern.at[0], k_f32.at[0], load_sem.at[2]),
+        pltpu.make_async_copy(kern.at[1], k_f32.at[1], load_sem.at[3]),
+        pltpu.make_async_copy(inv_in, inv, load_sem.at[4]),
+    ]
+    loads[0].start()
+    loads[1].start()
+
+    barrier = pltpu.get_barrier_semaphore()
+    for step in pts_steps:
+        pl.semaphore_signal(
+            barrier, inc=1, device_id=(me_s, pts_peer[step]), device_id_type=MESH
+        )
+    for step in sens_steps:
+        pl.semaphore_signal(
+            barrier, inc=1, device_id=(sens_peer[step], me_p), device_id_type=MESH
+        )
+
     started = []
 
-    def send_pts(*args):
-        for step in pts_steps:
-            copy = over_pts(step, *args)
-            copy.start()
-            started.append(copy)
-
-    def send_sens(*args):
-        for step in sens_steps:
-            copy = over_sens(step, *args)
-            copy.start()
-            started.append(copy)
-
-    nb = raw.shape[1]
+    def copy_pts(step, src, dst, send_sem, recv_sem):
+        return pltpu.make_async_remote_copy(
+            src_ref=src, dst_ref=dst, send_sem=send_sem.at[step], recv_sem=recv_sem.at[step],
+            device_id=(me_s, pts_peer[step]), device_id_type=MESH,
+        )
+
+    def copy_sens(step, slot, src, dst, send_sem, recv_sem):
+        at = slot * n_sens + step
+        return pltpu.make_async_remote_copy(
+            src_ref=src, dst_ref=dst, send_sem=send_sem.at[at], recv_sem=recv_sem.at[at],
+            device_id=(sens_peer[step], me_p), device_id_type=MESH,
+        )
+
+    def go(copy):
+        copy.start()
+        started.append(copy)
+
+    nb = raw.shape[0]
     pack[me_p] = jnp.zeros(pack.shape[1:], F32)
-    raw_t = jnp.transpose(raw[...])
+    raw_t = raw[...]
     pack[me_p, 0:nb, 0:ple] = raw_t / jnp.sum(raw_t, axis=0, keepdims=True)
     pack[me_p, nb : nb + 1, 0:ple] = amp[...]
-    pack[me_p, 0:nb, ple : 2 * ple] = jnp.transpose(offs[...].astype(F32))
+    pack[me_p, 0:nb, ple : 2 * ple] = offs[...].astype(F32)
 
     v_pad[...] = jnp.zeros(v_pad.shape, F32)
-    v_pad[:, 0:length] = vec[me_s]
     loads[0].wait()
-    source = dot3(v_pad[...], fwd[0], fwd[1])
-    for index in range(n_pts):
-        a_send[index] = source[:, index * cfp : (index + 1) * cfp]
-
+    v_pad[:, 0:length] = v_own[...]
+    loads[1].wait()
+    for load in loads[2:]:
+        load.start()
     pl.semaphore_wait(barrier, n_pts - 1 + n_sens - 1)
-    pack_args = (lambda _: pack.at[me_p], lambda i: pack.at[i], pack_s, pack_r)
-    send_pts(*pack_args)
-    a_args = (lambda i: a_send.at[i], lambda i: a_recv.at[i], a_s, a_r)
-    send_pts(*a_args)
-    a_recv[me_p] = a_send[me_p]
-
-    loads[1].wait()
+
+    for step in pts_steps:
+        go(copy_pts(step, pack.at[me_p], pack.at[me_p], pack_s, pack_r))
+
+    high, low = split(v_pad[...])
+    both = jnp.concatenate([high, low], axis=0)
+    for turn in list(range(1, pairs)) + [0]:
+        pair = pair_peer[turn]
+        part = jnp.dot(both, fwd[0, pair], preferred_element_type=F32)
+        source = part[:ple] + part[ple:] + jnp.dot(high, fwd[1, pair], preferred_element_type=F32)
+        for side in range(2):
+            a_send[2 * pair + side] = source[:, side * cfp : (side + 1) * cfp]
+        for step in (2 * turn, 2 * turn + 1):
+            if step:
+                go(copy_pts(step, a_send.at[pts_peer[step]], x_all.at[me_s, me_p], a_s, a_r))
+    x_all[me_s, me_p] = a_send[me_p]
+
+    def hand_on(step):
+        for other in sens_steps:
+            block = x_all.at[me_s, pts_peer[step]]
+            go(copy_sens(other, step, block, block, f_s, f_r))
+
+    hand_on(0)
+
     loads[2].wait()
+    loads[3].wait()
 
     def halve(index, carry):
         for part in range(2):
@@ -289,12 +301,18 @@
             k_hl[index, (2 + part) * sl : (3 + part) * sl] = low
         return carry
 
-    lax.fori_loop(0, fb, halve, 0)
+    share = -(-fb // (n_pts - 1))
+    for step in pts_steps:
+        lax.fori_loop(min((step - 1) * share, fb), min(step * share, fb), halve, 0, unroll=2)
+        block = x_all.at[me_s, pts_peer[step]]
+        copy_pts(step, block, block, a_s, a_r).wait_recv()
+        hand_on(step)
     for index in range(fb, fbp):
         k_hl[index] = jnp.zeros(k_hl.shape[1:], BF)
 
     for step in pts_steps:
-        arrive_pts(step, *pack_args)
+        block = pack.at[pts_peer[step]]
+        copy_pts(step, block, block, pack_s, pack_r).wait_recv()
     gathered = [pack[index] for index in range(n_pts)]
     weights_row = jnp.concatenate([block[:, 0:ple] for block in gathered], axis=1)
     offsets_row = jnp.concatenate([block[:, ple : 2 * ple] for block in gathered], axis=1)
@@ -316,20 +334,18 @@
     prior_t = total * weights_row[nb : nb + 1]
     prior_h, prior_l = split(prior_t)
 
-    for step in pts_steps:
-        arrive_pts(step, *a_args)
-    by_point = a_recv[...].reshape(pt, cfp)
-    own = dot3(jnp.transpose(by_point), prior_h, prior_l)
-    tiles = pt // 128
-    for part in range(2):
-        for tile in range(tiles):
-            spec[part, me_s, tile] = own[
-                part * fbp : (part + 1) * fbp, tile * 128 : (tile + 1) * 128
-            ]
-    s_args = (lambda _: spec.at[:, me_s], lambda i: spec.at[:, i], s_s, s_r)
-    send_sens(*s_args)
-    for step in sens_steps:
-        arrive_sens(step, *s_args)
+    for other in range(n_sens):
+        v = sens_peer[other]
+        if other:
+            for step in range(n_pts):
+                block = x_all.at[v, pts_peer[step]]
+                copy_sens(other, step, block, block, f_s, f_r).wait_recv()
+        own = dot3(jnp.transpose(x_all[v].reshape(pt, cfp)), prior_h, prior_l)
+        for part in range(2):
+            for tile in range(tiles):
+                spec[part, v, tile] = own[
+                    part * fbp : (part + 1) * fbp, tile * 128 : (tile + 1) * 128
+                ]
 
     spec_rows = spec.reshape(rows * tiles * fbp, 128)
 
@@ -362,28 +378,46 @@
         data = jnp.transpose(direct + pltpu.roll(crossed, sl, 1))
         for index in range(n_pts):
             d_send[index, v] = data[index * sq : (index + 1) * sq]
-    d_args = (lambda i: d_send.at[i], lambda i: d_recv.at[i], d_s, d_r)
-    send_pts(*d_args)
+    for step in reversed(pts_steps):
+        go(copy_pts(step, d_send.at[pts_peer[step]], d_recv.at[me_p], d_s, d_r))
     d_recv[me_p] = d_send[me_p]
-    loads[3].wait()
+    loads[4].wait()
     which = lax.rem(lax.broadcasted_iota(jnp.int32, (nv * sq, 1), 0), sq)
     precision = jnp.zeros((nv * sq, 1), F32)
     for index in range(sq):
         precision = jnp.where(which == index, noise[index], precision)
-    for step in pts_steps:
-        arrive_pts(step, *d_args)
-    data_spec = jnp.concatenate(
-        [d_recv[index].reshape(nv * sq, cfp) for index in range(n_pts)], axis=1
-    )
-    data = dot3(data_spec, inv[0], inv[1]) * precision
-    back = dot3(data, fwd[0], fwd[1])
-    for index in range(n_pts):
-        e_send[index] = back[:, index * cfp : (index + 1) * cfp].reshape(nv, sq, cfp)
-    e_args = (lambda i: e_send.at[i], lambda i: e_recv.at[i], e_s, e_r)
-    send_pts(*e_args)
+
+    def series(received, lines, send_sem, recv_sem):
+        result = jnp.zeros((lines, tp), F32)
+        for turn in range(pairs):
+            for step in (2 * turn, 2 * turn + 1):
+                if step:
+                    block = received.at[pts_peer[step]]
+                    copy_pts(step, block, block, send_sem, recv_sem).wait_recv()
+            pair = pair_peer[turn]
+            both = jnp.concatenate(
+                [received[2 * pair + side].reshape(lines, cfp) for side in range(2)], axis=1
+            )
+            result = result + dot3(both, inv[0, pair], inv[1, pair])
+        return result
+
+    data = series(d_recv, nv * sq, d_s, d_r) * precision
+    high, low = split(data)
+    both = jnp.concatenate([high, low], axis=0)
+    lines = nv * sq
+    for turn in list(range(1, pairs)) + [0]:
+        pair = pair_peer[turn]
+        part = jnp.dot(both, fwd[0, pair], preferred_element_type=F32)
+        back = part[:lines] + part[lines:] + jnp.dot(high, fwd[1, pair], preferred_element_type=F32)
+        for side in range(2):
+            e_send[2 * pair + side] = back[:, side * cfp : (side + 1) * cfp].reshape(nv, sq, cfp)
+        for step in (2 * turn, 2 * turn + 1):
+            if step:
+                go(copy_pts(step, e_send.at[pts_peer[step]], e_recv.at[me_p], e_s, e_r))
     e_recv[me_p] = e_send[me_p]
     for step in pts_steps:
-        arrive_pts(step, *e_args)
+        block = e_recv.at[pts_peer[step]]
+        copy_pts(step, block, block, e_s, e_r).wait_recv()
     for v in range(nv):
         turned = jnp.transpose(
             jnp.concatenate([e_recv[index, v] for index in range(n_pts)], axis=0)
@@ -413,14 +447,25 @@
             ]
         return carry
 
-    lax.fori_loop(0, fbp, adjoint, 0, unroll=8)
-
-    g_args = (lambda i: g_buf.at[:, i], lambda i: r_recv.at[i], g_s, g_r)
-    send_sens(*g_args)
+    groups = [(at, min(16, fbp - at)) for at in range(0, fbp, 16)]
+    for slot, (at, count) in enumerate(groups):
+        lax.fori_loop(at, at + count, adjoint, 0, unroll=8)
+        for step in reversed(sens_steps):
+            go(
+                copy_sens(
+                    step, slot,
+                    g_buf.at[:, sens_peer[step], :, pl.ds(at, count), :],
+                    r_recv.at[me_s, :, :, pl.ds(at, count), :],
+                    g_s, g_r,
+                )
+            )
     gradient = g_buf[:, me_s]
+    for slot, (at, count) in enumerate(groups):
+        for step in sens_steps:
+            block = r_recv.at[sens_peer[step], :, :, pl.ds(at, count), :]
+            copy_sens(step, slot, block, block, g_s, g_r).wait_recv()
     for step in sens_steps:
-        arrive_sens(step, *g_args)
-        gradient = gradient + r_recv[lax.rem(me_s - step + n_sens, n_sens)]
+        gradient = gradient + r_recv[sens_peer[step]]
     gradient = jnp.concatenate(
         [
             jnp.concatenate([gradient[part, tile] for tile in range(tiles)], axis=1)
@@ -431,20 +476,17 @@
     )
     grad_h, grad_l = split(gradient)
     h_send[...] = dot3(prior_t, grad_h, grad_l, NT).reshape(h_send.shape)
-    h_args = (lambda i: h_send.at[i], lambda i: h_recv.at[i], h_s, h_r)
-    send_pts(*h_args)
+    for step in reversed(pts_steps):
+        go(copy_pts(step, h_send.at[pts_peer[step]], h_recv.at[me_p], h_s, h_r))
     h_recv[me_p] = h_send[me_p]
-    for step in pts_steps:
-        arrive_pts(step, *h_args)
-    last = jnp.concatenate([h_recv[index] for index in range(n_pts)], axis=1)
-    o_buf[me_s] = dot3(last, inv[0], inv[1])
-    o_args = (lambda _: o_buf.at[me_s], lambda i: o_buf.at[i], o_s, o_r)
-    send_sens(*o_args)
-    out[me_s] = vec[me_s] + o_buf[me_s, :, 0:length]
+    o_buf[me_s] = series(h_recv, ple, h_s, h_r)
+    for step in reversed(sens_steps):
+        go(copy_sens(step, 0, o_buf.at[me_s], o_buf.at[me_s], o_s, o_r))
+    out[me_s] = o_buf[me_s, :, 0:length]
     for step in sens_steps:
-        arrive_sens(step, *o_args)
-        other = lax.rem(me_s - step + n_sens, n_sens)
-        out[other] = vec[other] + o_buf[other, :, 0:length]
+        block = o_buf.at[sens_peer[step]]
+        copy_sens(step, 0, block, block, o_s, o_r).wait_recv()
+        out[sens_peer[step]] = o_buf[sens_peer[step], :, 0:length]
     for copy in started:
         copy.wait_send()
 
@@ -461,6 +503,8 @@
     fits = (
         nv == n_sens
         and 2 * nv == 8
+        and n_pts & (n_pts - 1) == 0
+        and n_pts > 1
         and nb < 8
         and ple % 8 == 0
         and 2 * ple <= 128
@@ -479,7 +523,6 @@
     vmem = pl.BlockSpec(memory_space=pltpu.VMEM)
     smem = pl.BlockSpec(memory_space=pltpu.SMEM)
     anywhere = pl.BlockSpec(memory_space=pl.ANY)
-    wide = n_pts * cfp
 
     def f32(*shape):
         return pltpu.VMEM(shape, F32)
@@ -487,20 +530,21 @@
     def sems(count):
         return pltpu.SemaphoreType.DMA((count,))
 
-    return pl.pallas_call(
+    gradient = pl.pallas_call(
         functools.partial(fused_kernel, sizes),
         out_shape=jax.ShapeDtypeStruct(vectors.shape, F32),
-        in_specs=[vmem, anywhere, smem, vmem, vmem, vmem, smem, anywhere, anywhere],
+        in_specs=[anywhere, anywhere, smem, vmem, vmem, vmem, smem, anywhere, anywhere],
         out_specs=vmem,
         scratch_shapes=[
-            pltpu.VMEM((2, tp, wide), BF),
-            pltpu.VMEM((2, wide, tp), BF),
+            pltpu.VMEM(forward.shape, BF),
+            pltpu.VMEM(inverse.shape, BF),
             f32(2, fb, sl, pt),
             pltpu.VMEM((fbp, 4 * sl, pt), BF),
+            f32(ple, length),
             f32(ple, tp),
             f32(n_pts, 8, 128),
             f32(n_pts, ple, cfp),
-            f32(n_pts, ple, cfp),
+            f32(nv, n_pts, ple, cfp),
             f32(2, nv, pt // 128, fbp, 128),
             f32(fbp, 2 * nv, 2 * sl),
             f32(n_pts, nv, sq, cfp),
@@ -513,11 +557,11 @@
             f32(n_pts, ple, cfp),
             f32(n_pts, ple, cfp),
             f32(nv, ple, tp),
-            sems(4),
+            sems(5),
             *[sems(n_pts)] * 4,
-            *[sems(n_sens)] * 2,
+            *[sems(n_pts * n_sens)] * 2,
             *[sems(n_pts)] * 4,
-            *[sems(n_sens)] * 2,
+            *[sems(up(fbp, 16) // 16 * n_sens)] * 2,
             *[sems(n_pts)] * 2,
             *[sems(n_sens)] * 2,
         ],
@@ -525,9 +569,10 @@
             collective_id=0, has_side_effects=True, vmem_limit_bytes=56 * 2**20
         ),
     )(
-        vectors, kernel_hat, noise_prec, stencil_coefficients_raw, offsets,
+        vectors, kernel_hat, noise_prec, stencil_coefficients_raw.T, offsets.T,
         amplitude.reshape(1, ple), cheb_coef, forward, inverse,
     )
+    return vectors + gradient
 
 
 def solution(mesh):

time: 57 us -> 50.6 us (0.89)
  local copies, waits for them, and re-layouts: 4.41 us -> 0.01 us
  Pallas kernels: 52.3 us -> 48.7 us
  other arithmetic: 0 us -> 1.69 us
    unnamed x3 -> x2, local copies, waits for them, and re-layouts: 4.41 us -> 0.01 us
    pallas_call x1, Pallas kernels: 52.3 us -> 48.7 us  [local(): pl.pallas_call(functools.partial(fused_kernel, sizes), out_shape=jax.Shap...]
    add x0 -> x1, other arithmetic: none -> 1.69 us  [local(): return vectors + gradient]
where the time goes in v1:
time: 50.6 us; the launch traced here: 50.4 us
  Pallas kernels  48.7 us (96%)
  other arithmetic  1.69 us (3%)
    pallas_call x1, Pallas kernels, local(): pl.pallas_call(functools.partial(fused_kernel, sizes), out_shape=jax.Shap...  48.7 us
    add x1, other arithmetic, local(): return vectors + gradient  1.69 us

profile of v1, /device:TPU:0, one launch (start us, length us, event | category | flops | bytes accessed | tf_op | source)
XLA Modules:
  0.0 50.4 jit_solution(15400999555536726016)
XLA Ops:
  0.0 0.0 copy-start
  0.0 48.7 %shard_map.91 = f32[4,32,420]{2,1,0:T(8,128)} custom-call(f32[4,32,420]{2,1,0:T(8,128)} %vec.1, f32[2,53,64,256]{3,2,1,0:T(8,128)} %kern.1, f32[8]{0:T(128)} %noise.1, f32[6,32]{1,0:T(8,128)} %bitcast.3, s32[6,32]{1,0:T(8,128)} %bitcast.4, f32[1,32]{1,0:T(1,128)} %bitcast.5, f32[5]{0:T(128)} %cheb.1, bf16[2,4,512,256]{3,2,1,0:T(8,128)(2,1)} %constant.4.clone.fwd_in, ...), custom_call_target="tpu_custom_call" | custom-call | tf_op jit(solution)/shard_map/pallas_call | solution.py:533
  48.7 0.0 copy-done
  48.7 1.7 %add.3 = f32[4,32,420]{2,1,0:T(8,128)} add(f32[4,32,420]{2,1,0:T(8,128)S(1)} %copy-done, f32[4,32,420]{2,1,0:T(8,128)} %shard_map.91) | non-fusion elementwise | flops 53760 | bytes 645120 | tf_op jit(solution)/shard_map/add | solution.py:575
Async XLA Ops:
  0.0 48.7 %copy-start = (f32[4,32,420]{2,1,0:T(8,128)S(1)}, f32[4,32,420]{2,1,0:T(8,128)}, u32[]{:S(2)}) copy-start(f32[4,32,420]{2,1,0:T(8,128)} %vec.1) | copy-start | bytes 645124

commit v2 on v1

--- a/solution.py
+++ b/solution.py
@@ -197,7 +197,7 @@
     sizes,
     vec, kern, noise, raw, offs, amp, cheb, fwd_in, inv_in,
     out,
-    fwd, inv, k_f32, k_hl, v_own, v_pad, pack, a_send, x_all, spec, y_buf, d_send, d_recv,
+    fwd, inv, k_f32, k_hl, kt_hl, v_own, v_pad, pack, a_send, x_all, spec, y_buf, d_send, d_recv,
     e_send, e_recv, l_buf, g_buf, r_recv, h_send, h_recv, o_buf,
     load_sem, pack_s, pack_r, a_s, a_r, f_s, f_r, d_s, d_r, e_s, e_r, g_s, g_r, h_s, h_r, o_s, o_r,
 ):
@@ -205,7 +205,6 @@
     me_s = lax.axis_index("sens")
     me_p = lax.axis_index("pts")
     rows = 2 * nv
-    tiles = pt // 128
     pairs = n_pts // 2
     my_pair = me_p // 2
     pts_steps = range(1, n_pts)
@@ -295,10 +294,16 @@
     loads[3].wait()
 
     def halve(index, carry):
-        for part in range(2):
-            high, low = split(k_f32[part, index])
-            k_hl[index, part * sl : (part + 1) * sl] = high
-            k_hl[index, (2 + part) * sl : (3 + part) * sl] = low
+        high, low = split(jnp.concatenate([k_f32[0, index], k_f32[1, index]], axis=0))
+        k_hl[index, 0 : 2 * sl] = high
+        k_hl[index, 2 * sl : 4 * sl] = low
+        return carry
+
+    def halve_turned(index, carry):
+        both = jnp.concatenate([k_f32[0, index], k_f32[1, index]], axis=0)
+        high, low = split(jnp.transpose(both))
+        kt_hl[index, :, 0 : 2 * sl] = high
+        kt_hl[index, :, 2 * sl : 4 * sl] = low
         return carry
 
     share = -(-fb // (n_pts - 1))
@@ -309,6 +314,7 @@
         hand_on(step)
     for index in range(fb, fbp):
         k_hl[index] = jnp.zeros(k_hl.shape[1:], BF)
+        kt_hl[index] = jnp.zeros(kt_hl.shape[1:], BF)
 
     for step in pts_steps:
         block = pack.at[pts_peer[step]]
@@ -342,45 +348,51 @@
                 copy_sens(other, step, block, block, f_s, f_r).wait_recv()
         own = dot3(jnp.transpose(x_all[v].reshape(pt, cfp)), prior_h, prior_l)
         for part in range(2):
-            for tile in range(tiles):
-                spec[part, v, tile] = own[
-                    part * fbp : (part + 1) * fbp, tile * 128 : (tile + 1) * 128
-                ]
-
-    spec_rows = spec.reshape(rows * tiles * fbp, 128)
-
-    def predict(index, carry):
-        values = jnp.concatenate(
-            [
-                spec_rows[pl.ds(tile * fbp + index, rows, stride=tiles * fbp), :]
-                for tile in range(tiles)
-            ],
-            axis=1,
-        )
-        high, low = split(values)
-        product = lax.dot_general(
-            jnp.concatenate([high, low], axis=0), k_hl[index], NT, preferred_element_type=F32
-        )
-        y_buf[index] = (
-            product[:rows, : 2 * sl] + product[rows:, : 2 * sl] + product[:rows, 2 * sl :]
-        )
-        return carry
-
-    lax.fori_loop(0, fbp, predict, 0, unroll=8)
-
-    y_rows = y_buf.reshape(fbp * rows, 2 * sl)
-    blank = jnp.zeros((cfp - 2 * fbp, 2 * sl), F32)
+            spec[part, v] = own[part * fbp : (part + 1) * fbp]
+
+    lane = lax.broadcasted_iota(jnp.int32, (1, 16 * rows), 1)
+    lane_of = lax.rem(lane, 8)
+    sign = jnp.where(lax.rem(lane // (8 * nv), 2) == 0, -1.0, 1.0).astype(F32)
+
+    def columns(values):
+        high = values.astype(BF).astype(F32)
+        return jnp.transpose(jnp.concatenate([high, values - high], axis=0)).astype(BF)
+
+    def keep_own(products):
+        kept = products[0]
+        for index in range(1, 8):
+            kept = jnp.where(lane_of == index, products[index], kept)
+        return kept + pltpu.roll(kept, 8 * rows, 1)
+
+    for group in range(fbp // 8):
+        at = 8 * group
+        weight = columns(
+            jnp.concatenate(
+                [spec[part, v, at : at + 8] for part in range(2) for v in range(nv)], axis=0
+            )
+        )
+        product = jnp.dot(
+            k_hl[at : at + 8].reshape(32 * sl, pt), weight, preferred_element_type=F32
+        ).reshape(8, 2, 2 * sl, 16 * rows)
+        kept = keep_own([product[index, 0] + product[index, 1] for index in range(8)])
+        data = kept[:sl] + sign * pltpu.roll(kept[sl:], 8 * nv, 1)
+        y_buf[group] = jnp.transpose(data)[: 8 * rows].reshape(rows, 8, sl)
+
+    blank = jnp.zeros((cfp - 2 * fbp, sl), F32)
     for v in range(nv):
-        real = y_rows[pl.ds(v, fbp, stride=rows), :]
-        imag = y_rows[pl.ds(nv + v, fbp, stride=rows), :]
-        direct = jnp.concatenate([real, imag, blank], axis=0)
-        crossed = jnp.concatenate([-imag, real, blank], axis=0)
-        data = jnp.transpose(direct + pltpu.roll(crossed, sl, 1))
+        data = jnp.transpose(
+            jnp.concatenate(
+                [y_buf[group, part * nv + v] for part in range(2) for group in range(fbp // 8)]
+                + [blank],
+                axis=0,
+            )
+        )
         for index in range(n_pts):
             d_send[index, v] = data[index * sq : (index + 1) * sq]
     for step in reversed(pts_steps):
         go(copy_pts(step, d_send.at[pts_peer[step]], d_recv.at[me_p], d_s, d_r))
     d_recv[me_p] = d_send[me_p]
+    lax.fori_loop(0, fb // 2, halve_turned, 0, unroll=2)
     loads[4].wait()
     which = lax.rem(lax.broadcasted_iota(jnp.int32, (nv * sq, 1), 0), sq)
     precision = jnp.zeros((nv * sq, 1), F32)
@@ -415,6 +427,7 @@
             if step:
                 go(copy_pts(step, e_send.at[pts_peer[step]], e_recv.at[me_p], e_s, e_r))
     e_recv[me_p] = e_send[me_p]
+    lax.fori_loop(fb // 2, fb, halve_turned, 0, unroll=2)
     for step in pts_steps:
         block = e_recv.at[pts_peer[step]]
         copy_pts(step, block, block, e_s, e_r).wait_recv()
@@ -426,53 +439,38 @@
         l_buf[0, v] = jnp.concatenate([real, imag], axis=1)
         l_buf[1, v] = jnp.concatenate([imag, -real], axis=1)
 
-    l_rows = l_buf.reshape(rows * fbp, 2 * sl)
-    g_rows = g_buf.reshape(rows * tiles * fbp, 128)
-
-    def adjoint(index, carry):
-        values = l_rows[pl.ds(index, rows, stride=fbp), :]
-        high, low = split(values)
-        left = jnp.concatenate(
-            [
-                jnp.concatenate([high, high], axis=1),
-                jnp.concatenate([low, jnp.zeros_like(low)], axis=1),
-            ],
-            axis=0,
-        )
-        product = lax.dot_general(left, k_hl[index], NN, preferred_element_type=F32)
-        result = product[:rows] + product[rows:]
-        for tile in range(tiles):
-            g_rows[pl.ds(tile * fbp + index, rows, stride=tiles * fbp), :] = result[
-                :, tile * 128 : (tile + 1) * 128
-            ]
-        return carry
-
     groups = [(at, min(16, fbp - at)) for at in range(0, fbp, 16)]
     for slot, (at, count) in enumerate(groups):
-        lax.fori_loop(at, at + count, adjoint, 0, unroll=8)
+        for first in range(at, at + count, 8):
+            weight = columns(l_buf[:, :, first : first + 8].reshape(8 * rows, 2 * sl))
+            product = jnp.dot(
+                kt_hl[first : first + 8].reshape(8 * pt, 4 * sl),
+                jnp.concatenate([weight, weight], axis=0),
+                preferred_element_type=F32,
+            ).reshape(8, pt, 16 * rows)
+            kept = jnp.transpose(keep_own([product[index] for index in range(8)]))
+            for part in range(2):
+                for v in range(nv):
+                    row = 8 * (part * nv + v)
+                    g_buf[part, v, first : first + 8] = kept[row : row + 8]
         for step in reversed(sens_steps):
             go(
                 copy_sens(
                     step, slot,
-                    g_buf.at[:, sens_peer[step], :, pl.ds(at, count), :],
-                    r_recv.at[me_s, :, :, pl.ds(at, count), :],
+                    g_buf.at[:, sens_peer[step], pl.ds(at, count), :],
+                    r_recv.at[me_s, :, pl.ds(at, count), :],
                     g_s, g_r,
                 )
             )
     gradient = g_buf[:, me_s]
     for slot, (at, count) in enumerate(groups):
         for step in sens_steps:
-            block = r_recv.at[sens_peer[step], :, :, pl.ds(at, count), :]
+            block = r_recv.at[sens_peer[step], :, pl.ds(at, count), :]
             copy_sens(step, slot, block, block, g_s, g_r).wait_recv()
     for step in sens_steps:
         gradient = gradient + r_recv[sens_peer[step]]
     gradient = jnp.concatenate(
-        [
-            jnp.concatenate([gradient[part, tile] for tile in range(tiles)], axis=1)
-            for part in range(2)
-        ]
-        + [jnp.zeros((cfp - 2 * fbp, pt), F32)],
-        axis=0,
+        [gradient.reshape(2 * fbp, pt), jnp.zeros((cfp - 2 * fbp, pt), F32)], axis=0
     )
     grad_h, grad_l = split(gradient)
     h_send[...] = dot3(prior_t, grad_h, grad_l, NT).reshape(h_send.shape)
@@ -540,20 +538,21 @@
             pltpu.VMEM(inverse.shape, BF),
             f32(2, fb, sl, pt),
             pltpu.VMEM((fbp, 4 * sl, pt), BF),
+            pltpu.VMEM((fbp, pt, 4 * sl), BF),
             f32(ple, length),
             f32(ple, tp),
             f32(n_pts, 8, 128),
             f32(n_pts, ple, cfp),
             f32(nv, n_pts, ple, cfp),
-            f32(2, nv, pt // 128, fbp, 128),
-            f32(fbp, 2 * nv, 2 * sl),
+            f32(2, nv, fbp, pt),
+            f32(fbp // 8, 2 * nv, 8, sl),
             f32(n_pts, nv, sq, cfp),
             f32(n_pts, nv, sq, cfp),
             f32(n_pts, nv, sq, cfp),
             f32(n_pts, nv, sq, cfp),
             f32(2, nv, fbp, 2 * sl),
-            f32(2, nv, pt // 128, fbp, 128),
-            f32(n_sens, 2, pt // 128, fbp, 128),
+            f32(2, nv, fbp, pt),
+            f32(n_sens, 2, fbp, pt),
             f32(n_pts, ple, cfp),
             f32(n_pts, ple, cfp),
             f32(nv, ple, tp),

time: 50.6 us -> 51 us (level)
  no operation moved by 1% of the time
where the time goes in v2:
time: 51 us; the launch traced here: 50.8 us
  Pallas kernels  49.1 us (96%)
  other arithmetic  1.69 us (3%)
    pallas_call x1, Pallas kernels, local(): pl.pallas_call(functools.partial(fused_kernel, sizes), out_shape=jax.Shap...  49.1 us
    add x1, other arithmetic, local(): return vectors + gradient  1.69 us

profile of v2, /device:TPU:0, one launch (start us, length us, event | category | flops | bytes accessed | tf_op | source)
XLA Modules:
  0.0 50.8 jit_solution(12106127203952017736)
XLA Ops:
  0.0 0.0 copy-start
  0.0 49.1 %shard_map.91 = f32[4,32,420]{2,1,0:T(8,128)} custom-call(f32[4,32,420]{2,1,0:T(8,128)} %vec.1, f32[2,53,64,256]{3,2,1,0:T(8,128)} %kern.1, f32[8]{0:T(128)} %noise.1, f32[6,32]{1,0:T(8,128)} %bitcast.3, s32[6,32]{1,0:T(8,128)} %bitcast.4, f32[1,32]{1,0:T(1,128)} %bitcast.5, f32[5]{0:T(128)} %cheb.1, bf16[2,4,512,256]{3,2,1,0:T(8,128)(2,1)} %constant.4.clone.fwd_in, ...), custom_call_target="tpu_custom_call" | custom-call | tf_op jit(solution)/shard_map/pallas_call | solution.py:531
  49.1 0.0 copy-done
  49.1 1.7 %add.3 = f32[4,32,420]{2,1,0:T(8,128)} add(f32[4,32,420]{2,1,0:T(8,128)S(1)} %copy-done, f32[4,32,420]{2,1,0:T(8,128)} %shard_map.91) | non-fusion elementwise | flops 53760 | bytes 645120 | tf_op jit(solution)/shard_map/add | solution.py:574
Async XLA Ops:
  0.0 49.1 %copy-start = (f32[4,32,420]{2,1,0:T(8,128)S(1)}, f32[4,32,420]{2,1,0:T(8,128)}, u32[]{:S(2)}) copy-start(f32[4,32,420]{2,1,0:T(8,128)} %vec.1) | copy-start | bytes 645124

commit v3 on v2

--- a/solution.py
+++ b/solution.py
@@ -161,7 +161,7 @@
     for table in (forward, inverse):
         high = table.astype(ml_dtypes.bfloat16)
         low = (table - high.astype(np.float64)).astype(ml_dtypes.bfloat16)
-        halves.append(np.stack([high, low]))
+        halves.append(np.stack([high, low], axis=1))
     return halves
 
 
@@ -197,31 +197,35 @@
     sizes,
     vec, kern, noise, raw, offs, amp, cheb, fwd_in, inv_in,
     out,
-    fwd, inv, k_f32, k_hl, kt_hl, v_own, v_pad, pack, a_send, x_all, spec, y_buf, d_send, d_recv,
-    e_send, e_recv, l_buf, g_buf, r_recv, h_send, h_recv, o_buf,
-    load_sem, pack_s, pack_r, a_s, a_r, f_s, f_r, d_s, d_r, e_s, e_r, g_s, g_r, h_s, h_r, o_s, o_r,
+    fwd, inv, k_f32, k_hl, kt_hl, v_in, v_pad, a_send, a_recv, b_send, x_all, spec, y_buf,
+    d_send, d_recv, e_send, e_recv, l_buf, g_buf, r_recv, h_send, h_recv, o_buf,
+    load_sem, fwd_sem, a_s, a_r, b_s, b_r, f_s, f_r, d_s, d_r, e_s, e_r, g_s, g_r, h_s, h_r, o_s, o_r,
 ):
     nv, n_sens, n_pts, fb, fbp, cfp, sl, sq, pt, ple, length, tp = sizes
     me_s = lax.axis_index("sens")
     me_p = lax.axis_index("pts")
     rows = 2 * nv
     pairs = n_pts // 2
-    my_pair = me_p // 2
     pts_steps = range(1, n_pts)
     sens_steps = range(1, n_sens)
+    far_first = list(range(pairs - 1, -1, -1))
     pts_peer = [flip(me_p, step, n_pts) for step in range(n_pts)]
     sens_peer = [flip(me_s, step, n_sens) for step in range(n_sens)]
-    pair_peer = [flip(my_pair, step, pairs) for step in range(pairs)]
-
-    loads = [
-        pltpu.make_async_copy(vec.at[me_s], v_own, load_sem.at[0]),
-        pltpu.make_async_copy(fwd_in, fwd, load_sem.at[1]),
-        pltpu.make_async_copy(kern.at[0], k_f32.at[0], load_sem.at[2]),
-        pltpu.make_async_copy(kern.at[1], k_f32.at[1], load_sem.at[3]),
-        pltpu.make_async_copy(inv_in, inv, load_sem.at[4]),
+    pair_peer = [flip(me_p // 2, step, pairs) for step in range(pairs)]
+
+    vec_load = pltpu.make_async_copy(vec, v_in, load_sem.at[0])
+    k_loads = [
+        pltpu.make_async_copy(kern.at[part], k_f32.at[part], load_sem.at[1 + part])
+        for part in range(2)
     ]
-    loads[0].start()
-    loads[1].start()
+    inv_load = pltpu.make_async_copy(inv_in, inv, load_sem.at[3])
+    fwd_loads = [
+        pltpu.make_async_copy(fwd_in.at[pair], fwd.at[pair], fwd_sem.at[turn])
+        for turn, pair in enumerate(pair_peer)
+    ]
+    vec_load.start()
+    for turn in far_first:
+        fwd_loads[turn].start()
 
     barrier = pltpu.get_barrier_semaphore()
     for step in pts_steps:
@@ -233,65 +237,84 @@
             barrier, inc=1, device_id=(sens_peer[step], me_p), device_id_type=MESH
         )
 
-    started = []
-
-    def copy_pts(step, src, dst, send_sem, recv_sem):
-        return pltpu.make_async_remote_copy(
-            src_ref=src, dst_ref=dst, send_sem=send_sem.at[step], recv_sem=recv_sem.at[step],
+    def to_pts(step, src, dst, send_sem, recv_sem):
+        pltpu.make_async_remote_copy(
+            src_ref=src, dst_ref=dst, send_sem=send_sem, recv_sem=recv_sem.at[step // 2],
             device_id=(me_s, pts_peer[step]), device_id_type=MESH,
-        )
-
-    def copy_sens(step, slot, src, dst, send_sem, recv_sem):
-        at = slot * n_sens + step
-        return pltpu.make_async_remote_copy(
-            src_ref=src, dst_ref=dst, send_sem=send_sem.at[at], recv_sem=recv_sem.at[at],
+        ).start()
+
+    def to_sens(step, src, dst, send_sem, recv_sem):
+        pltpu.make_async_remote_copy(
+            src_ref=src, dst_ref=dst, send_sem=send_sem, recv_sem=recv_sem.at[step],
             device_id=(sens_peer[step], me_p), device_id_type=MESH,
-        )
-
-    def go(copy):
-        copy.start()
-        started.append(copy)
+        ).start()
+
+    def wait(block, semaphore):
+        pltpu.make_async_copy(block, block, semaphore).wait()
+
+    def wait_pair(turn, received, semaphore):
+        if turn:
+            wait(received.at[pl.ds(2 * pair_peer[turn], 2)], semaphore.at[turn])
+        else:
+            wait(received.at[pts_peer[1]], semaphore.at[0])
 
     nb = raw.shape[0]
-    pack[me_p] = jnp.zeros(pack.shape[1:], F32)
     raw_t = raw[...]
-    pack[me_p, 0:nb, 0:ple] = raw_t / jnp.sum(raw_t, axis=0, keepdims=True)
-    pack[me_p, nb : nb + 1, 0:ple] = amp[...]
-    pack[me_p, 0:nb, ple : 2 * ple] = offs[...].astype(F32)
+    pack = jnp.concatenate(
+        [
+            jnp.concatenate(
+                [raw_t / jnp.sum(raw_t, axis=0, keepdims=True), offs[...].astype(F32)], axis=1
+            ),
+            jnp.concatenate([amp[...], amp[...]], axis=1),
+            jnp.zeros((7 - nb, 2 * ple), F32),
+        ],
+        axis=0,
+    )
+    for index in range(n_pts):
+        a_send[index, ple:] = jnp.zeros((8, cfp), F32)
+        a_send[index, ple:, 0 : 2 * ple] = pack
 
     v_pad[...] = jnp.zeros(v_pad.shape, F32)
-    loads[0].wait()
-    v_pad[:, 0:length] = v_own[...]
-    loads[1].wait()
-    for load in loads[2:]:
+    vec_load.wait()
+    v_pad[:, :, 0:length] = v_in[...]
+
+    def transformed(values, pair, lines):
+        high, low = split(values)
+        both = jnp.concatenate([high, low], axis=0)
+        part = jnp.dot(both, fwd[pair, 0], preferred_element_type=F32)
+        return (
+            part[:lines] + part[lines:]
+            + jnp.dot(high, fwd[pair, 1], preferred_element_type=F32)
+        )
+
+    mine = v_pad[me_s]
+    for turn in far_first:
+        pair = pair_peer[turn]
+        fwd_loads[turn].wait()
+        if turn == pairs - 1:
+            pl.semaphore_wait(barrier, n_pts - 1 + n_sens - 1)
+        if turn:
+            source = transformed(mine, pair, ple)
+            for side in range(2):
+                a_send[2 * pair + side, 0:ple] = source[:, side * cfp : (side + 1) * cfp]
+            for step in (2 * turn, 2 * turn + 1):
+                to_pts(step, a_send.at[pts_peer[step]], a_recv.at[me_p], a_s, a_r)
+    for load in k_loads:
         load.start()
-    pl.semaphore_wait(barrier, n_pts - 1 + n_sens - 1)
-
-    for step in pts_steps:
-        go(copy_pts(step, pack.at[me_p], pack.at[me_p], pack_s, pack_r))
-
-    high, low = split(v_pad[...])
-    both = jnp.concatenate([high, low], axis=0)
-    for turn in list(range(1, pairs)) + [0]:
-        pair = pair_peer[turn]
-        part = jnp.dot(both, fwd[0, pair], preferred_element_type=F32)
-        source = part[:ple] + part[ple:] + jnp.dot(high, fwd[1, pair], preferred_element_type=F32)
-        for side in range(2):
-            a_send[2 * pair + side] = source[:, side * cfp : (side + 1) * cfp]
-        for step in (2 * turn, 2 * turn + 1):
-            if step:
-                go(copy_pts(step, a_send.at[pts_peer[step]], x_all.at[me_s, me_p], a_s, a_r))
-    x_all[me_s, me_p] = a_send[me_p]
-
-    def hand_on(step):
-        for other in sens_steps:
-            block = x_all.at[me_s, pts_peer[step]]
-            go(copy_sens(other, step, block, block, f_s, f_r))
-
-    hand_on(0)
-
-    loads[2].wait()
-    loads[3].wait()
+    inv_load.start()
+    source = transformed(v_pad[...].reshape(nv * ple, tp), pair_peer[0], nv * ple)
+    for side in range(2):
+        b_send[side] = source[:, side * cfp : (side + 1) * cfp].reshape(nv, ple, cfp)
+    other_side = lax.rem(pts_peer[1], 2)
+    to_pts(1, b_send.at[other_side], x_all.at[:, me_p], b_s.at[0], b_r)
+    to_pts(1, a_send.at[pts_peer[1], ple:], a_recv.at[me_p, ple:], b_s.at[1], a_r)
+    own_side = lax.rem(me_p, 2)
+    for v in range(nv):
+        x_all[v, me_p] = b_send[own_side, v]
+    a_recv[me_p, ple:] = a_send[me_p, ple:]
+
+    for load in k_loads:
+        load.wait()
 
     def halve(index, carry):
         high, low = split(jnp.concatenate([k_f32[0, index], k_f32[1, index]], axis=0))
@@ -306,20 +329,27 @@
         kt_hl[index, :, 2 * sl : 4 * sl] = low
         return carry
 
-    share = -(-fb // (n_pts - 1))
-    for step in pts_steps:
-        lax.fori_loop(min((step - 1) * share, fb), min(step * share, fb), halve, 0, unroll=2)
-        block = x_all.at[me_s, pts_peer[step]]
-        copy_pts(step, block, block, a_s, a_r).wait_recv()
-        hand_on(step)
+    share = -(-fb // pairs)
+    for turn in list(range(1, pairs)) + [0]:
+        first = (turn - 1 if turn else pairs - 1) * share
+        lax.fori_loop(min(first, fb), min(first + share, fb), halve, 0, unroll=2)
+        if turn:
+            wait_pair(turn, a_recv, a_r)
+            span = pl.ds(2 * pair_peer[turn], 2)
+            for step in sens_steps:
+                to_sens(
+                    step, a_recv.at[span, 0:ple], x_all.at[me_s, span], f_s, f_r
+                )
+            for side in range(2):
+                at = 2 * pair_peer[turn] + side
+                x_all[me_s, at] = a_recv[at, 0:ple]
+        else:
+            wait(a_recv.at[pts_peer[1], ple:], a_r.at[0])
     for index in range(fb, fbp):
         k_hl[index] = jnp.zeros(k_hl.shape[1:], BF)
         kt_hl[index] = jnp.zeros(kt_hl.shape[1:], BF)
 
-    for step in pts_steps:
-        block = pack.at[pts_peer[step]]
-        copy_pts(step, block, block, pack_s, pack_r).wait_recv()
-    gathered = [pack[index] for index in range(n_pts)]
+    gathered = [a_recv[index, ple:] for index in range(n_pts)]
     weights_row = jnp.concatenate([block[:, 0:ple] for block in gathered], axis=1)
     offsets_row = jnp.concatenate([block[:, ple : 2 * ple] for block in gathered], axis=1)
     down = lax.broadcasted_iota(jnp.int32, (pt, pt), 0)
@@ -340,12 +370,11 @@
     prior_t = total * weights_row[nb : nb + 1]
     prior_h, prior_l = split(prior_t)
 
+    wait(x_all.at[:, pts_peer[1]], b_r.at[0])
     for other in range(n_sens):
         v = sens_peer[other]
         if other:
-            for step in range(n_pts):
-                block = x_all.at[v, pts_peer[step]]
-                copy_sens(other, step, block, block, f_s, f_r).wait_recv()
+            wait(x_all.at[v, pl.ds(0, n_pts - 2)], f_r.at[other])
         own = dot3(jnp.transpose(x_all[v].reshape(pt, cfp)), prior_h, prior_l)
         for part in range(2):
             spec[part, v] = own[part * fbp : (part + 1) * fbp]
@@ -390,47 +419,39 @@
         for index in range(n_pts):
             d_send[index, v] = data[index * sq : (index + 1) * sq]
     for step in reversed(pts_steps):
-        go(copy_pts(step, d_send.at[pts_peer[step]], d_recv.at[me_p], d_s, d_r))
+        to_pts(step, d_send.at[pts_peer[step]], d_recv.at[me_p], d_s, d_r)
     d_recv[me_p] = d_send[me_p]
     lax.fori_loop(0, fb // 2, halve_turned, 0, unroll=2)
-    loads[4].wait()
+    inv_load.wait()
     which = lax.rem(lax.broadcasted_iota(jnp.int32, (nv * sq, 1), 0), sq)
     precision = jnp.zeros((nv * sq, 1), F32)
     for index in range(sq):
         precision = jnp.where(which == index, noise[index], precision)
 
-    def series(received, lines, send_sem, recv_sem):
+    def series(received, lines, recv_sem):
         result = jnp.zeros((lines, tp), F32)
         for turn in range(pairs):
-            for step in (2 * turn, 2 * turn + 1):
-                if step:
-                    block = received.at[pts_peer[step]]
-                    copy_pts(step, block, block, send_sem, recv_sem).wait_recv()
+            wait_pair(turn, received, recv_sem)
             pair = pair_peer[turn]
             both = jnp.concatenate(
                 [received[2 * pair + side].reshape(lines, cfp) for side in range(2)], axis=1
             )
-            result = result + dot3(both, inv[0, pair], inv[1, pair])
+            result = result + dot3(both, inv[pair, 0], inv[pair, 1])
         return result
 
-    data = series(d_recv, nv * sq, d_s, d_r) * precision
-    high, low = split(data)
-    both = jnp.concatenate([high, low], axis=0)
-    lines = nv * sq
-    for turn in list(range(1, pairs)) + [0]:
+    data = series(d_recv, nv * sq, d_r) * precision
+    for turn in far_first:
         pair = pair_peer[turn]
-        part = jnp.dot(both, fwd[0, pair], preferred_element_type=F32)
-        back = part[:lines] + part[lines:] + jnp.dot(high, fwd[1, pair], preferred_element_type=F32)
+        back = transformed(data, pair, nv * sq)
         for side in range(2):
             e_send[2 * pair + side] = back[:, side * cfp : (side + 1) * cfp].reshape(nv, sq, cfp)
-        for step in (2 * turn, 2 * turn + 1):
+        for step in (2 * turn + 1, 2 * turn):
             if step:
-                go(copy_pts(step, e_send.at[pts_peer[step]], e_recv.at[me_p], e_s, e_r))
+                to_pts(step, e_send.at[pts_peer[step]], e_recv.at[me_p], e_s, e_r)
     e_recv[me_p] = e_send[me_p]
     lax.fori_loop(fb // 2, fb, halve_turned, 0, unroll=2)
-    for step in pts_steps:
-        block = e_recv.at[pts_peer[step]]
-        copy_pts(step, block, block, e_s, e_r).wait_recv()
+    for turn in range(pairs):
+        wait_pair(turn, e_recv, e_r)
     for v in range(nv):
         turned = jnp.transpose(
             jnp.concatenate([e_recv[index, v] for index in range(n_pts)], axis=0)
@@ -439,8 +460,8 @@
         l_buf[0, v] = jnp.concatenate([real, imag], axis=1)
         l_buf[1, v] = jnp.concatenate([imag, -real], axis=1)
 
-    groups = [(at, min(16, fbp - at)) for at in range(0, fbp, 16)]
-    for slot, (at, count) in enumerate(groups):
+    groups = [(at, min(24, fbp - at)) for at in range(0, fbp, 24)]
+    for at, count in groups:
         for first in range(at, at + count, 8):
             weight = columns(l_buf[:, :, first : first + 8].reshape(8 * rows, 2 * sl))
             product = jnp.dot(
@@ -454,20 +475,15 @@
                     row = 8 * (part * nv + v)
                     g_buf[part, v, first : first + 8] = kept[row : row + 8]
         for step in reversed(sens_steps):
-            go(
-                copy_sens(
-                    step, slot,
-                    g_buf.at[:, sens_peer[step], pl.ds(at, count), :],
-                    r_recv.at[me_s, :, pl.ds(at, count), :],
-                    g_s, g_r,
-                )
+            to_sens(
+                step,
+                g_buf.at[:, sens_peer[step], pl.ds(at, count), :],
+                r_recv.at[me_s, :, pl.ds(at, count), :],
+                g_s, g_r,
             )
     gradient = g_buf[:, me_s]
-    for slot, (at, count) in enumerate(groups):
-        for step in sens_steps:
-            block = r_recv.at[sens_peer[step], :, pl.ds(at, count), :]
-            copy_sens(step, slot, block, block, g_s, g_r).wait_recv()
     for step in sens_steps:
+        wait(r_recv.at[sens_peer[step]], g_r.at[step])
         gradient = gradient + r_recv[sens_peer[step]]
     gradient = jnp.concatenate(
         [gradient.reshape(2 * fbp, pt), jnp.zeros((cfp - 2 * fbp, pt), F32)], axis=0
@@ -475,18 +491,24 @@
     grad_h, grad_l = split(gradient)
     h_send[...] = dot3(prior_t, grad_h, grad_l, NT).reshape(h_send.shape)
     for step in reversed(pts_steps):
-        go(copy_pts(step, h_send.at[pts_peer[step]], h_recv.at[me_p], h_s, h_r))
+        to_pts(step, h_send.at[pts_peer[step]], h_recv.at[me_p], h_s, h_r)
     h_recv[me_p] = h_send[me_p]
-    o_buf[me_s] = series(h_recv, ple, h_s, h_r)
+    o_buf[me_s] = series(h_recv, ple, h_r)
     for step in reversed(sens_steps):
-        go(copy_sens(step, 0, o_buf.at[me_s], o_buf.at[me_s], o_s, o_r))
+        to_sens(step, o_buf.at[me_s], o_buf.at[me_s], o_s, o_r)
     out[me_s] = o_buf[me_s, :, 0:length]
     for step in sens_steps:
-        block = o_buf.at[sens_peer[step]]
-        copy_sens(step, 0, block, block, o_s, o_r).wait_recv()
+        wait(o_buf.at[sens_peer[step]], o_r.at[step])
         out[sens_peer[step]] = o_buf[sens_peer[step], :, 0:length]
-    for copy in started:
-        copy.wait_send()
+
+    wait(a_send.at[pl.ds(0, n_pts - 2)], a_s)
+    wait(b_send.at[0], b_s.at[0])
+    wait(a_send.at[0, ple:], b_s.at[1])
+    wait(x_all.at[pl.ds(0, n_sens - 1), pl.ds(0, n_pts - 2)], f_s)
+    for sent, semaphore in ((d_send, d_s), (e_send, e_s), (h_send, h_s)):
+        wait(sent.at[pl.ds(0, n_pts - 1)], semaphore)
+    wait(r_recv.at[pl.ds(0, n_sens - 1)], g_s)
+    wait(o_buf.at[pl.ds(0, n_sens - 1)], o_s)
 
 
 def local(vectors, kernel_hat, noise_prec, stencil_coefficients_raw, offsets, amplitude, cheb_coef):
@@ -502,8 +524,8 @@
         nv == n_sens
         and 2 * nv == 8
         and n_pts & (n_pts - 1) == 0
-        and n_pts > 1
         and nb < 8
+        and n_pts > 2
         and ple % 8 == 0
         and 2 * ple <= 128
         and sl == sq * n_pts
@@ -528,6 +550,7 @@
     def sems(count):
         return pltpu.SemaphoreType.DMA((count,))
 
+    one = pltpu.SemaphoreType.DMA
     gradient = pl.pallas_call(
         functools.partial(fused_kernel, sizes),
         out_shape=jax.ShapeDtypeStruct(vectors.shape, F32),
@@ -539,10 +562,11 @@
             f32(2, fb, sl, pt),
             pltpu.VMEM((fbp, 4 * sl, pt), BF),
             pltpu.VMEM((fbp, pt, 4 * sl), BF),
-            f32(ple, length),
-            f32(ple, tp),
-            f32(n_pts, 8, 128),
-            f32(n_pts, ple, cfp),
+            f32(nv, ple, length),
+            f32(nv, ple, tp),
+            f32(n_pts, ple + 8, cfp),
+            f32(n_pts, ple + 8, cfp),
+            f32(2, nv, ple, cfp),
             f32(nv, n_pts, ple, cfp),
             f32(2, nv, fbp, pt),
             f32(fbp // 8, 2 * nv, 8, sl),
@@ -556,13 +580,24 @@
             f32(n_pts, ple, cfp),
             f32(n_pts, ple, cfp),
             f32(nv, ple, tp),
-            sems(5),
-            *[sems(n_pts)] * 4,
-            *[sems(n_pts * n_sens)] * 2,
-            *[sems(n_pts)] * 4,
-            *[sems(up(fbp, 16) // 16 * n_sens)] * 2,
-            *[sems(n_pts)] * 2,
-            *[sems(n_sens)] * 2,
+            sems(4),
+            sems(n_pts // 2),
+            one,
+            sems(n_pts // 2),
+            sems(2),
+            sems(n_pts // 2),
+            one,
+            sems(n_sens),
+            one,
+            sems(n_pts // 2),
+            one,
+            sems(n_pts // 2),
+            one,
+            sems(n_sens),
+            one,
+            sems(n_pts // 2),
+            one,
+            sems(n_sens),
         ],
         compiler_params=pltpu.CompilerParams(
             collective_id=0, has_side_effects=True, vmem_limit_bytes=56 * 2**20

time: 51 us -> 51 us (level)
  no operation moved by 1% of the time
where the time goes in v3:
time: 51 us; the launch traced here: 50.8 us
  Pallas kernels  49.1 us (96%)
  other arithmetic  1.69 us (3%)
    pallas_call x1, Pallas kernels, local(): pl.pallas_call(functools.partial(fused_kernel, sizes), out_shape=jax.Shap...  49.1 us
    add x1, other arithmetic, local(): return vectors + gradient  1.69 us

profile of v3, /device:TPU:0, one launch (start us, length us, event | category | flops | bytes accessed | tf_op | source)
XLA Modules:
  0.0 50.8 jit_solution(18204371157258973743)
XLA Ops:
  0.0 0.0 copy-start
  0.0 49.1 %shard_map.91 = f32[4,32,420]{2,1,0:T(8,128)} custom-call(f32[4,32,420]{2,1,0:T(8,128)} %vec.1, f32[2,53,64,256]{3,2,1,0:T(8,128)} %kern.1, f32[8]{0:T(128)} %noise.1, f32[6,32]{1,0:T(8,128)} %bitcast.3, s32[6,32]{1,0:T(8,128)} %bitcast.4, f32[1,32]{1,0:T(1,128)} %bitcast.5, f32[5]{0:T(128)} %cheb.1, bf16[4,2,512,256]{3,2,1,0:T(8,128)(2,1)} %constant.4.clone.fwd_in, ...), custom_call_target="tpu_custom_call" | custom-call | tf_op jit(solution)/shard_map/pallas_call | solution.py:554
  49.1 0.0 copy-done
  49.1 1.7 %add.3 = f32[4,32,420]{2,1,0:T(8,128)} add(f32[4,32,420]{2,1,0:T(8,128)S(1)} %copy-done, f32[4,32,420]{2,1,0:T(8,128)} %shard_map.91) | non-fusion elementwise | flops 53760 | bytes 645120 | tf_op jit(solution)/shard_map/add | solution.py:609
Async XLA Ops:
  0.0 49.1 %copy-start = (f32[4,32,420]{2,1,0:T(8,128)S(1)}, f32[4,32,420]{2,1,0:T(8,128)}, u32[]{:S(2)}) copy-start(f32[4,32,420]{2,1,0:T(8,128)} %vec.1) | copy-start | bytes 645124

commit v4 on v3

--- a/solution.py
+++ b/solution.py
@@ -197,9 +197,9 @@
     sizes,
     vec, kern, noise, raw, offs, amp, cheb, fwd_in, inv_in,
     out,
-    fwd, inv, k_f32, k_hl, kt_hl, v_in, v_pad, a_send, a_recv, b_send, x_all, spec, y_buf,
+    fwd, inv, k_f32, k_hl, v_in, v_pad, a_send, a_recv, b_send, x_all, spec, y_buf,
     d_send, d_recv, e_send, e_recv, l_buf, g_buf, r_recv, h_send, h_recv, o_buf,
-    load_sem, fwd_sem, a_s, a_r, b_s, b_r, f_s, f_r, d_s, d_r, e_s, e_r, g_s, g_r, h_s, h_r, o_s, o_r,
+    load_sem, k_sem, fwd_sem, a_s, a_r, b_s, b_r, f_s, f_r, d_s, d_r, e_s, e_r, g_s, g_r, h_s, h_r, o_s, o_r,
 ):
     nv, n_sens, n_pts, fb, fbp, cfp, sl, sq, pt, ple, length, tp = sizes
     me_s = lax.axis_index("sens")
@@ -214,11 +214,15 @@
     pair_peer = [flip(me_p // 2, step, pairs) for step in range(pairs)]
 
     vec_load = pltpu.make_async_copy(vec, v_in, load_sem.at[0])
+    share = -(-fb // n_pts)
+    k_spans = [(at, min(share, fb - at)) for at in range(0, fb, share)]
     k_loads = [
-        pltpu.make_async_copy(kern.at[part], k_f32.at[part], load_sem.at[1 + part])
-        for part in range(2)
+        pltpu.make_async_copy(
+            kern.at[:, pl.ds(at, count)], k_f32.at[:, pl.ds(at, count)], k_sem.at[index]
+        )
+        for index, (at, count) in enumerate(k_spans)
     ]
-    inv_load = pltpu.make_async_copy(inv_in, inv, load_sem.at[3])
+    inv_load = pltpu.make_async_copy(inv_in, inv, load_sem.at[1])
     fwd_loads = [
         pltpu.make_async_copy(fwd_in.at[pair], fwd.at[pair], fwd_sem.at[turn])
         for turn, pair in enumerate(pair_peer)
@@ -292,6 +296,9 @@
         pair = pair_peer[turn]
         fwd_loads[turn].wait()
         if turn == pairs - 1:
+            for load in k_loads:
+                load.start()
+            inv_load.start()
             pl.semaphore_wait(barrier, n_pts - 1 + n_sens - 1)
         if turn:
             source = transformed(mine, pair, ple)
@@ -299,9 +306,6 @@
                 a_send[2 * pair + side, 0:ple] = source[:, side * cfp : (side + 1) * cfp]
             for step in (2 * turn, 2 * turn + 1):
                 to_pts(step, a_send.at[pts_peer[step]], a_recv.at[me_p], a_s, a_r)
-    for load in k_loads:
-        load.start()
-    inv_load.start()
     source = transformed(v_pad[...].reshape(nv * ple, tp), pair_peer[0], nv * ple)
     for side in range(2):
         b_send[side] = source[:, side * cfp : (side + 1) * cfp].reshape(nv, ple, cfp)
@@ -313,26 +317,20 @@
         x_all[v, me_p] = b_send[own_side, v]
     a_recv[me_p, ple:] = a_send[me_p, ple:]
 
-    for load in k_loads:
-        load.wait()
-
     def halve(index, carry):
         high, low = split(jnp.concatenate([k_f32[0, index], k_f32[1, index]], axis=0))
         k_hl[index, 0 : 2 * sl] = high
         k_hl[index, 2 * sl : 4 * sl] = low
         return carry
 
-    def halve_turned(index, carry):
-        both = jnp.concatenate([k_f32[0, index], k_f32[1, index]], axis=0)
-        high, low = split(jnp.transpose(both))
-        kt_hl[index, :, 0 : 2 * sl] = high
-        kt_hl[index, :, 2 * sl : 4 * sl] = low
-        return carry
-
-    share = -(-fb // pairs)
+    def halve_span(index):
+        at, count = k_spans[index]
+        k_loads[index].wait()
+        lax.fori_loop(at, at + count, halve, 0, unroll=True)
+
     for turn in list(range(1, pairs)) + [0]:
-        first = (turn - 1 if turn else pairs - 1) * share
-        lax.fori_loop(min(first, fb), min(first + share, fb), halve, 0, unroll=2)
+        if turn:
+            halve_span(turn - 1)
         if turn:
             wait_pair(turn, a_recv, a_r)
             span = pl.ds(2 * pair_peer[turn], 2)
@@ -347,7 +345,6 @@
             wait(a_recv.at[pts_peer[1], ple:], a_r.at[0])
     for index in range(fb, fbp):
         k_hl[index] = jnp.zeros(k_hl.shape[1:], BF)
-        kt_hl[index] = jnp.zeros(kt_hl.shape[1:], BF)
 
     gathered = [a_recv[index, ple:] for index in range(n_pts)]
     weights_row = jnp.concatenate([block[:, 0:ple] for block in gathered], axis=1)
@@ -373,6 +370,9 @@
     wait(x_all.at[:, pts_peer[1]], b_r.at[0])
     for other in range(n_sens):
         v = sens_peer[other]
+        if other == 1:
+            for index in range(pairs - 1, len(k_spans)):
+                halve_span(index)
         if other:
             wait(x_all.at[v, pl.ds(0, n_pts - 2)], f_r.at[other])
         own = dot3(jnp.transpose(x_all[v].reshape(pt, cfp)), prior_h, prior_l)
@@ -421,7 +421,6 @@
     for step in reversed(pts_steps):
         to_pts(step, d_send.at[pts_peer[step]], d_recv.at[me_p], d_s, d_r)
     d_recv[me_p] = d_send[me_p]
-    lax.fori_loop(0, fb // 2, halve_turned, 0, unroll=2)
     inv_load.wait()
     which = lax.rem(lax.broadcasted_iota(jnp.int32, (nv * sq, 1), 0), sq)
     precision = jnp.zeros((nv * sq, 1), F32)
@@ -449,7 +448,6 @@
             if step:
                 to_pts(step, e_send.at[pts_peer[step]], e_recv.at[me_p], e_s, e_r)
     e_recv[me_p] = e_send[me_p]
-    lax.fori_loop(fb // 2, fb, halve_turned, 0, unroll=2)
     for turn in range(pairs):
         wait_pair(turn, e_recv, e_r)
     for v in range(nv):
@@ -460,25 +458,35 @@
         l_buf[0, v] = jnp.concatenate([real, imag], axis=1)
         l_buf[1, v] = jnp.concatenate([imag, -real], axis=1)
 
+    tiles = pt // 128
+    l_rows = l_buf.reshape(rows * fbp, 2 * sl)
+    g_rows = g_buf.reshape(rows * tiles * fbp, 128)
+
+    def adjoint(index, carry):
+        high, low = split(l_rows[pl.ds(index, rows, stride=fbp), :])
+        left = jnp.concatenate(
+            [
+                jnp.concatenate([high, high], axis=1),
+                jnp.concatenate([low, jnp.zeros_like(low)], axis=1),
+            ],
+            axis=0,
+        )
+        product = jnp.dot(left, k_hl[index], preferred_element_type=F32)
+        result = product[:rows] + product[rows:]
+        for tile in range(tiles):
+            g_rows[pl.ds(tile * fbp + index, rows, stride=tiles * fbp), :] = result[
+                :, tile * 128 : (tile + 1) * 128
+            ]
+        return carry
+
     groups = [(at, min(24, fbp - at)) for at in range(0, fbp, 24)]
     for at, count in groups:
-        for first in range(at, at + count, 8):
-            weight = columns(l_buf[:, :, first : first + 8].reshape(8 * rows, 2 * sl))
-            product = jnp.dot(
-                kt_hl[first : first + 8].reshape(8 * pt, 4 * sl),
-                jnp.concatenate([weight, weight], axis=0),
-                preferred_element_type=F32,
-            ).reshape(8, pt, 16 * rows)
-            kept = jnp.transpose(keep_own([product[index] for index in range(8)]))
-            for part in range(2):
-                for v in range(nv):
-                    row = 8 * (part * nv + v)
-                    g_buf[part, v, first : first + 8] = kept[row : row + 8]
+        lax.fori_loop(at, at + count, adjoint, 0, unroll=8)
         for step in reversed(sens_steps):
             to_sens(
                 step,
-                g_buf.at[:, sens_peer[step], pl.ds(at, count), :],
-                r_recv.at[me_s, :, pl.ds(at, count), :],
+                g_buf.at[:, sens_peer[step], :, pl.ds(at, count), :],
+                r_recv.at[me_s, :, :, pl.ds(at, count), :],
                 g_s, g_r,
             )
     gradient = g_buf[:, me_s]
@@ -486,7 +494,12 @@
         wait(r_recv.at[sens_peer[step]], g_r.at[step])
         gradient = gradient + r_recv[sens_peer[step]]
     gradient = jnp.concatenate(
-        [gradient.reshape(2 * fbp, pt), jnp.zeros((cfp - 2 * fbp, pt), F32)], axis=0
+        [
+            jnp.concatenate([gradient[part, tile] for tile in range(tiles)], axis=1)
+            for part in range(2)
+        ]
+        + [jnp.zeros((cfp - 2 * fbp, pt), F32)],
+        axis=0,
     )
     grad_h, grad_l = split(gradient)
     h_send[...] = dot3(prior_t, grad_h, grad_l, NT).reshape(h_send.shape)
@@ -526,6 +539,7 @@
         and n_pts & (n_pts - 1) == 0
         and nb < 8
         and n_pts > 2
+        and fb >= n_pts
         and ple % 8 == 0
         and 2 * ple <= 128
         and sl == sq * n_pts
@@ -561,7 +575,6 @@
             pltpu.VMEM(inverse.shape, BF),
             f32(2, fb, sl, pt),
             pltpu.VMEM((fbp, 4 * sl, pt), BF),
-            pltpu.VMEM((fbp, pt, 4 * sl), BF),
             f32(nv, ple, length),
             f32(nv, ple, tp),
             f32(n_pts, ple + 8, cfp),
@@ -575,12 +588,13 @@
             f32(n_pts, nv, sq, cfp),
             f32(n_pts, nv, sq, cfp),
             f32(2, nv, fbp, 2 * sl),
-            f32(2, nv, fbp, pt),
-            f32(n_sens, 2, fbp, pt),
+            f32(2, nv, pt // 128, fbp, 128),
+            f32(n_sens, 2, pt // 128, fbp, 128),
             f32(n_pts, ple, cfp),
             f32(n_pts, ple, cfp),
             f32(nv, ple, tp),
-            sems(4),
+            sems(2),
+            sems(n_pts),
             sems(n_pts // 2),
             one,
             sems(n_pts // 2),

time: 51 us -> 49.6 us (0.973)
  Pallas kernels: 49.1 us -> 47.7 us
    pallas_call x1, Pallas kernels: 49.1 us -> 47.7 us  [local(): pl.pallas_call(functools.partial(fused_kernel, sizes), out_shape=jax.Shap...]
where the time goes in v4:
time: 49.6 us; the launch traced here: 49.4 us
  Pallas kernels  47.7 us (96%)
  other arithmetic  1.69 us (3%)
    pallas_call x1, Pallas kernels, local(): pl.pallas_call(functools.partial(fused_kernel, sizes), out_shape=jax.Shap...  47.7 us
    add x1, other arithmetic, local(): return vectors + gradient  1.69 us

profile of v4, /device:TPU:0, one launch (start us, length us, event | category | flops | bytes accessed | tf_op | source)
XLA Modules:
  0.0 49.4 jit_solution(12553258018245420642)
XLA Ops:
  0.0 0.0 copy-start
  0.0 47.7 %shard_map.91 = f32[4,32,420]{2,1,0:T(8,128)} custom-call(f32[4,32,420]{2,1,0:T(8,128)} %vec.1, f32[2,53,64,256]{3,2,1,0:T(8,128)} %kern.1, f32[8]{0:T(128)} %noise.1, f32[6,32]{1,0:T(8,128)} %bitcast.3, s32[6,32]{1,0:T(8,128)} %bitcast.4, f32[1,32]{1,0:T(1,128)} %bitcast.5, f32[5]{0:T(128)} %cheb.1, bf16[4,2,512,256]{3,2,1,0:T(8,128)(2,1)} %constant.4.clone.fwd_in, ...), custom_call_target="tpu_custom_call" | custom-call | tf_op jit(solution)/shard_map/pallas_call | solution.py:568
  47.7 0.0 copy-done
  47.7 1.7 %add.3 = f32[4,32,420]{2,1,0:T(8,128)} add(f32[4,32,420]{2,1,0:T(8,128)S(1)} %copy-done, f32[4,32,420]{2,1,0:T(8,128)} %shard_map.91) | non-fusion elementwise | flops 53760 | bytes 645120 | tf_op jit(solution)/shard_map/add | solution.py:623
Async XLA Ops:
  0.0 47.7 %copy-start = (f32[4,32,420]{2,1,0:T(8,128)S(1)}, f32[4,32,420]{2,1,0:T(8,128)}, u32[]{:S(2)}) copy-start(f32[4,32,420]{2,1,0:T(8,128)} %vec.1) | copy-start | bytes 645124

commit v5 on v4

--- a/solution.py
+++ b/solution.py
@@ -195,11 +195,11 @@
 
 def fused_kernel(
     sizes,
-    vec, kern, noise, raw, offs, amp, cheb, fwd_in, inv_in,
+    vec, kern, noise_in, raw_in, offs_in, amp_in, cheb_in, fwd_in, inv_in,
     out,
-    fwd, inv, k_f32, k_hl, v_in, v_pad, a_send, a_recv, b_send, x_all, spec, y_buf,
+    noise, raw, offs, amp, cheb, fwd, inv, k_f32, k_hl, v_in, v_pad, a_send, a_recv, b_send, x_all, spec, y_buf,
     d_send, d_recv, e_send, e_recv, l_buf, g_buf, r_recv, h_send, h_recv, o_buf,
-    load_sem, k_sem, fwd_sem, a_s, a_r, b_s, b_r, f_s, f_r, d_s, d_r, e_s, e_r, g_s, g_r, h_s, h_r, o_s, o_r,
+    small_sem, load_sem, k_sem, fwd_sem, a_s, a_r, b_s, b_r, f_s, f_r, d_s, d_r, e_s, e_r, g_s, g_r, h_s, h_r, o_s, o_r,
 ):
     nv, n_sens, n_pts, fb, fbp, cfp, sl, sq, pt, ple, length, tp = sizes
     me_s = lax.axis_index("sens")
@@ -227,7 +227,15 @@
         pltpu.make_async_copy(fwd_in.at[pair], fwd.at[pair], fwd_sem.at[turn])
         for turn, pair in enumerate(pair_peer)
     ]
+    small_loads = [
+        pltpu.make_async_copy(there, here, small_sem.at[index])
+        for index, (there, here) in enumerate(
+            ((raw_in, raw), (offs_in, offs), (amp_in, amp), (noise_in, noise), (cheb_in, cheb))
+        )
+    ]
     vec_load.start()
+    for load in small_loads:
+        load.start()
     for turn in far_first:
         fwd_loads[turn].start()
 
@@ -262,6 +270,8 @@
         else:
             wait(received.at[pts_peer[1]], semaphore.at[0])
 
+    for load in small_loads:
+        load.wait()
     nb = raw.shape[0]
     raw_t = raw[...]
     pack = jnp.concatenate(
@@ -368,16 +378,25 @@
     prior_h, prior_l = split(prior_t)
 
     wait(x_all.at[:, pts_peer[1]], b_r.at[0])
-    for other in range(n_sens):
-        v = sens_peer[other]
-        if other == 1:
-            for index in range(pairs - 1, len(k_spans)):
-                halve_span(index)
-        if other:
-            wait(x_all.at[v, pl.ds(0, n_pts - 2)], f_r.at[other])
-        own = dot3(jnp.transpose(x_all[v].reshape(pt, cfp)), prior_h, prior_l)
-        for part in range(2):
-            spec[part, v] = own[part * fbp : (part + 1) * fbp]
+
+    def field_spectra(vectors_now):
+        own = dot3(
+            jnp.concatenate(
+                [jnp.transpose(x_all[v].reshape(pt, cfp)) for v in vectors_now], axis=0
+            ),
+            prior_h, prior_l,
+        )
+        for index, v in enumerate(vectors_now):
+            for part in range(2):
+                at = index * cfp + part * fbp
+                spec[part, v] = own[at : at + fbp]
+
+    field_spectra([me_s])
+    for index in range(pairs - 1, len(k_spans)):
+        halve_span(index)
+    for step in sens_steps:
+        wait(x_all.at[sens_peer[step], pl.ds(0, n_pts - 2)], f_r.at[step])
+    field_spectra(sens_peer[1:])
 
     lane = lax.broadcasted_iota(jnp.int32, (1, 16 * rows), 1)
     lane_of = lax.rem(lane, 8)
@@ -479,9 +498,10 @@
             ]
         return carry
 
-    groups = [(at, min(24, fbp - at)) for at in range(0, fbp, 24)]
+    cuts = [0] + list(range(8, fbp, 16)) + [fbp]
+    groups = [(at, after - at) for at, after in zip(cuts, cuts[1:])]
     for at, count in groups:
-        lax.fori_loop(at, at + count, adjoint, 0, unroll=8)
+        lax.fori_loop(at, at + count, adjoint, 0, unroll=True)
         for step in reversed(sens_steps):
             to_sens(
                 step,
@@ -555,7 +575,6 @@
     forward, inverse = host_tables(length, fb, n_pts, fbp, cfp, tp)
     sizes = (nv, n_sens, n_pts, fb, fbp, cfp, sl, sq, pt, ple, length, tp)
     vmem = pl.BlockSpec(memory_space=pltpu.VMEM)
-    smem = pl.BlockSpec(memory_space=pltpu.SMEM)
     anywhere = pl.BlockSpec(memory_space=pl.ANY)
 
     def f32(*shape):
@@ -568,9 +587,14 @@
     gradient = pl.pallas_call(
         functools.partial(fused_kernel, sizes),
         out_shape=jax.ShapeDtypeStruct(vectors.shape, F32),
-        in_specs=[anywhere, anywhere, smem, vmem, vmem, vmem, smem, anywhere, anywhere],
+        in_specs=[anywhere] * 9,
         out_specs=vmem,
         scratch_shapes=[
+            pltpu.SMEM(noise_prec.shape, F32),
+            f32(nb, ple),
+            pltpu.VMEM((nb, ple), jnp.int32),
+            f32(1, ple),
+            pltpu.SMEM(cheb_coef.shape, F32),
             pltpu.VMEM(forward.shape, BF),
             pltpu.VMEM(inverse.shape, BF),
             f32(2, fb, sl, pt),
@@ -593,6 +617,7 @@
             f32(n_pts, ple, cfp),
             f32(n_pts, ple, cfp),
             f32(nv, ple, tp),
+            sems(5),
             sems(2),
             sems(n_pts),
             sems(n_pts // 2),

time: 49.6 us -> 48.9 us (0.986)
  Pallas kernels: 47.7 us -> 47.1 us
    pallas_call x1, Pallas kernels: 47.7 us -> 47.1 us  [local(): pl.pallas_call(functools.partial(fused_kernel, sizes), out_shape=jax.Shap...]
where the time goes in v5:
time: 48.9 us; the launch traced here: 48.8 us
  Pallas kernels  47.1 us (96%)
  other arithmetic  1.69 us (3%)
    pallas_call x1, Pallas kernels, local(): pl.pallas_call(functools.partial(fused_kernel, sizes), out_shape=jax.Shap...  47.1 us
    add x1, other arithmetic, local(): return vectors + gradient  1.69 us

profile of v5, /device:TPU:0, one launch (start us, length us, event | category | flops | bytes accessed | tf_op | source)
XLA Modules:
  0.0 48.8 jit_solution(16549537056284418191)
XLA Ops:
  0.0 0.0 copy-start
  0.0 47.1 %shard_map.91 = f32[4,32,420]{2,1,0:T(8,128)} custom-call(f32[4,32,420]{2,1,0:T(8,128)} %vec.1, f32[2,53,64,256]{3,2,1,0:T(8,128)} %kern.1, f32[8]{0:T(128)} %noise_in.1, f32[6,32]{1,0:T(8,128)} %bitcast.3, s32[6,32]{1,0:T(8,128)} %bitcast.4, f32[1,32]{1,0:T(1,128)} %bitcast.5, f32[5]{0:T(128)} %cheb_in.1, bf16[4,2,512,256]{3,2,1,0:T(8,128)(2,1)} %constant.4.clone.fwd_in, ...), custom_call_target="tpu_custom_call" | custom-call | tf_op jit(solution)/shard_map/pallas_call | solution.py:587
  47.1 0.0 copy-done
  47.1 1.7 %add.3 = f32[4,32,420]{2,1,0:T(8,128)} add(f32[4,32,420]{2,1,0:T(8,128)S(1)} %copy-done, f32[4,32,420]{2,1,0:T(8,128)} %shard_map.91) | non-fusion elementwise | flops 53760 | bytes 645120 | tf_op jit(solution)/shard_map/add | solution.py:648
Async XLA Ops:
  0.0 47.1 %copy-start = (f32[4,32,420]{2,1,0:T(8,128)S(1)}, f32[4,32,420]{2,1,0:T(8,128)}, u32[]{:S(2)}) copy-start(f32[4,32,420]{2,1,0:T(8,128)} %vec.1) | copy-start | bytes 645124

commit v6 on v5

--- a/solution.py
+++ b/solution.py
@@ -199,7 +199,7 @@
     out,
     noise, raw, offs, amp, cheb, fwd, inv, k_f32, k_hl, v_in, v_pad, a_send, a_recv, b_send, x_all, spec, y_buf,
     d_send, d_recv, e_send, e_recv, l_buf, g_buf, r_recv, h_send, h_recv, o_buf,
-    small_sem, load_sem, k_sem, fwd_sem, a_s, a_r, b_s, b_r, f_s, f_r, d_s, d_r, e_s, e_r, g_s, g_r, h_s, h_r, o_s, o_r,
+    small_sem, load_sem, k_sem, fwd_sem, a_s, a_r, b_s, b_r, f_s, f_r, d_s, d_r, e_s, e_r, g_s, g_r, h_s, h_r, h_r_late, o_s, o_r,
 ):
     nv, n_sens, n_pts, fb, fbp, cfp, sl, sq, pt, ple, length, tp = sizes
     me_s = lax.axis_index("sens")
@@ -264,11 +264,11 @@
     def wait(block, semaphore):
         pltpu.make_async_copy(block, block, semaphore).wait()
 
-    def wait_pair(turn, received, semaphore):
+    def wait_pair(turn, received, semaphore, part=slice(None)):
         if turn:
-            wait(received.at[pl.ds(2 * pair_peer[turn], 2)], semaphore.at[turn])
+            wait(received.at[pl.ds(2 * pair_peer[turn], 2), part], semaphore.at[turn])
         else:
-            wait(received.at[pts_peer[1]], semaphore.at[0])
+            wait(received.at[pts_peer[1], part], semaphore.at[0])
 
     for load in small_loads:
         load.wait()
@@ -446,13 +446,13 @@
     for index in range(sq):
         precision = jnp.where(which == index, noise[index], precision)
 
-    def series(received, lines, recv_sem):
+    def series(received, lines, recv_sem, part=slice(None)):
         result = jnp.zeros((lines, tp), F32)
         for turn in range(pairs):
-            wait_pair(turn, received, recv_sem)
+            wait_pair(turn, received, recv_sem, part)
             pair = pair_peer[turn]
             both = jnp.concatenate(
-                [received[2 * pair + side].reshape(lines, cfp) for side in range(2)], axis=1
+                [received[2 * pair + side, part].reshape(lines, cfp) for side in range(2)], axis=1
             )
             result = result + dot3(both, inv[pair, 0], inv[pair, 1])
         return result
@@ -523,12 +523,15 @@
     )
     grad_h, grad_l = split(gradient)
     h_send[...] = dot3(prior_t, grad_h, grad_l, NT).reshape(h_send.shape)
-    for step in reversed(pts_steps):
-        to_pts(step, h_send.at[pts_peer[step]], h_recv.at[me_p], h_s, h_r)
+    halves = [(pl.ds(at, ple // 2), sem) for at, sem in ((0, h_r), (ple // 2, h_r_late))]
+    for part, semaphore in halves:
+        for step in reversed(pts_steps):
+            to_pts(step, h_send.at[pts_peer[step], part], h_recv.at[me_p, part], h_s, semaphore)
     h_recv[me_p] = h_send[me_p]
-    o_buf[me_s] = series(h_recv, ple, h_r)
-    for step in reversed(sens_steps):
-        to_sens(step, o_buf.at[me_s], o_buf.at[me_s], o_s, o_r)
+    for part, semaphore in halves:
+        o_buf[me_s, part] = series(h_recv, ple // 2, semaphore, part)
+        for step in reversed(sens_steps):
+            to_sens(step, o_buf.at[me_s, part], o_buf.at[me_s, part], o_s, o_r)
     out[me_s] = o_buf[me_s, :, 0:length]
     for step in sens_steps:
         wait(o_buf.at[sens_peer[step]], o_r.at[step])
@@ -560,7 +563,7 @@
         and nb < 8
         and n_pts > 2
         and fb >= n_pts
-        and ple % 8 == 0
+        and ple % 32 == 0
         and 2 * ple <= 128
         and sl == sq * n_pts
         and sq % 8 == 0
@@ -635,6 +638,7 @@
             sems(n_sens),
             one,
             sems(n_pts // 2),
+            sems(n_pts // 2),
             one,
             sems(n_sens),
         ],

time: 48.9 us -> 49 us (level)
  no operation moved by 1% of the time
where the time goes in v6:
time: 49 us; the launch traced here: 48.8 us
  Pallas kernels  47.1 us (96%)
  other arithmetic  1.69 us (3%)
    pallas_call x1, Pallas kernels, local(): pl.pallas_call(functools.partial(fused_kernel, sizes), out_shape=jax.Shap...  47.1 us
    add x1, other arithmetic, local(): return vectors + gradient  1.69 us

profile of v6, /device:TPU:0, one launch (start us, length us, event | category | flops | bytes accessed | tf_op | source)
XLA Modules:
  0.0 48.8 jit_solution(6718180464392937014)
XLA Ops:
  0.0 0.0 copy-start
  0.0 47.1 %shard_map.91 = f32[4,32,420]{2,1,0:T(8,128)} custom-call(f32[4,32,420]{2,1,0:T(8,128)} %vec.1, f32[2,53,64,256]{3,2,1,0:T(8,128)} %kern.1, f32[8]{0:T(128)} %noise_in.1, f32[6,32]{1,0:T(8,128)} %bitcast.3, s32[6,32]{1,0:T(8,128)} %bitcast.4, f32[1,32]{1,0:T(1,128)} %bitcast.5, f32[5]{0:T(128)} %cheb_in.1, bf16[4,2,512,256]{3,2,1,0:T(8,128)(2,1)} %constant.4.clone.fwd_in, ...), custom_call_target="tpu_custom_call" | custom-call | tf_op jit(solution)/shard_map/pallas_call | solution.py:590
  47.1 0.0 copy-done
  47.1 1.7 %add.3 = f32[4,32,420]{2,1,0:T(8,128)} add(f32[4,32,420]{2,1,0:T(8,128)S(1)} %copy-done, f32[4,32,420]{2,1,0:T(8,128)} %shard_map.91) | non-fusion elementwise | flops 53760 | bytes 645120 | tf_op jit(solution)/shard_map/add | solution.py:652
Async XLA Ops:
  0.0 47.1 %copy-start = (f32[4,32,420]{2,1,0:T(8,128)S(1)}, f32[4,32,420]{2,1,0:T(8,128)}, u32[]{:S(2)}) copy-start(f32[4,32,420]{2,1,0:T(8,128)} %vec.1) | copy-start | bytes 645124
